TPU v7x, 256 devices: a whole 4x4x8 slice. The times are simulated.
256 devices in a mesh: rep: 16 (over x, z_lo), filt: 16 (over z_hi, y, core).
Axes of the slice: x: 4, y: 4, z: 8 (z_hi: 2, z_lo: 4; z = z_hi * 4 + z_lo), core: 2. Of those that a mesh axis runs over, the one named last changes fastest.
Arguments:
- images: bfloat16 [2016, 16, 224], P('filt', 'rep'), may hold values from -6 to 6
- labels: int32 [16], P('rep'), may hold values from 0 to 999
- partner: int32 [16], replicated, may hold values from 0 to 15, as said below
- student_w3: bfloat16 [16, 2016, 9, 1008], P('rep', 'filt'), may hold values from -0.0625 to 0.0625
- student_w1: bfloat16 [16, 2016, 2016], P('rep', 'filt'), may hold values from -0.125 to 0.125
- student_head: bfloat16 [16, 2016, 1000], P('rep', 'filt')
- stale_w3: bfloat16 [16, 2016, 9, 1008], P('rep', 'filt'), may hold values from -0.0625 to 0.0625
- stale_w1: bfloat16 [16, 2016, 2016], P('rep', 'filt'), may hold values from -0.125 to 0.125
- stale_head: bfloat16 [16, 2016, 1000], P('rep', 'filt')
Outputs:
- grad_w3: float32 [16, 2016, 9, 1008], P('rep', 'filt')
- grad_w1: float32 [16, 2016, 2016], P('rep', 'filt')
- grad_head: float32 [16, 2016, 1000], P('rep', 'filt')
Inputs may be any that keep to these rules, and one draw needn't show every extreme that they name: Replicas are paired both ways: partner[partner[r]] = r, no replica is its own partner, and partner[r] = r XOR partner[0] for every r.
All inputs are finite; a program needn't handle non-finite values.
Results may differ from a plain program's by a relative error of at most 0.0083.
Values may be sent and summed in bfloat16 or wider, within the bound.
A program may use at most 128 MiB of HBM per device.

v0:
```python
import jax
import jax.numpy as jnp
from jax import lax
from jax.sharding import PartitionSpec as P

C = 2016
GW = 1008
K = 1000
ROWS = 4
MAP_W = 56


def swapped(block, axis, bit):
    count = lax.axis_size(axis)
    route = []
    for low in range(count):
        high = low | 1 << bit
        if high != low and high < count:
            route += [(low, high), (high, low)]
    return lax.ppermute(block, axis, route)


def dsilu(values):
    sig = jax.nn.sigmoid(values)
    return sig * (1.0 + values * (1.0 - sig))


def tap_stack(panel):
    chans, count = (panel.shape[0], panel.shape[1])
    grid = panel.reshape(chans, count, ROWS, MAP_W)
    padded = jnp.pad(grid, ((0, 0), (0, 0), (1, 1), (1, 1)))
    taps = [
        padded[:, :, row_off : row_off + ROWS, col_off : col_off + MAP_W].reshape(
            chans, count * ROWS * MAP_W
        )
        for row_off in range(3)
        for col_off in range(3)
    ]
    return jnp.stack(taps).reshape(9 * chans, count * ROWS * MAP_W)


def group_tap_list(full_panel):
    groups = C // GW
    return [tap_stack(full_panel[group::groups]) for group in range(groups)]


def grouped_pre(group_taps, conv_w3):
    groups = C // GW
    local_chans = conv_w3.shape[0]
    pieces = []
    for group in range(groups):
        weights = conv_w3[group::groups].reshape(local_chans // groups, 9 * GW)
        pieces.append(jnp.dot(weights, group_taps[group], preferred_element_type=jnp.float32))
    pre = jnp.stack(pieces, axis=1).reshape(local_chans, -1)
    return (pre, jax.nn.silu(pre).astype(jnp.bfloat16))


def pooled_logits(inputs, z_mixed, classifier):
    local_chans, count = (inputs.shape[0], inputs.shape[1])
    pooled = jax.nn.silu(z_mixed).reshape(local_chans, count, ROWS * MAP_W).mean(axis=2)
    return (
        pooled,
        jnp.dot(pooled.T, classifier.astype(jnp.float32), precision=lax.Precision.HIGHEST),
    )


def teacher_tail(inputs, hidden, conv_w1, classifier):
    local_chans = inputs.shape[0]
    start_total = inputs.reshape(local_chans, -1).astype(jnp.float32)
    z_mixed = start_total + jnp.dot(
        conv_w1,
        lax.all_gather(hidden, "filt", axis=0, tiled=True),
        preferred_element_type=jnp.float32,
    )
    return pooled_logits(inputs, z_mixed, classifier)[1]


def sum_logits(student_part, teacher_part):
    return lax.psum((student_part, teacher_part), "filt")


def per_device(
    images, labels, partner, student_w3, student_w1, student_head, stale_w3, stale_w1, stale_head
):
    groups = C // GW
    local_chans = images.shape[0]
    columns_count = images.shape[1] * images.shape[2]
    replica_id = lax.axis_index("rep")
    pair_mask = jnp.bitwise_xor(
        lax.dynamic_index_in_dim(partner, replica_id, 0, keepdims=False), replica_id
    )
    levels = lax.axis_size("rep").bit_length() - 1

    def route(payload, mover):
        for bit_level in range(levels):
            moved = mover(payload, bit_level)
            chosen = jnp.bitwise_and(jnp.right_shift(pair_mask, bit_level), 1) == 1
            payload = jax.tree.map(
                lambda kept_leaf, moved_leaf: jnp.where(chosen, moved_leaf, kept_leaf),
                payload,
                moved,
            )
        return payload

    own_w3, own_w1, own_head = (student_w3[0], student_w1[0], student_head[0])
    full_panel = lax.all_gather(images, "filt", axis=0, tiled=True)
    group_taps = group_tap_list(full_panel)
    pre, hidden = grouped_pre(group_taps, own_w3)
    full_hidden = lax.all_gather(hidden, "filt", axis=0, tiled=True)
    z_mixed = images.reshape(local_chans, -1).astype(jnp.float32) + jnp.dot(
        own_w1, full_hidden, preferred_element_type=jnp.float32
    )
    pooled, student_part = pooled_logits(images, z_mixed, own_head)

    def swap_weights(payload, bit_level):
        return jax.tree.map(lambda tensor_leaf: swapped(tensor_leaf, "rep", bit_level), payload)

    teach_w3, teach_w1, teach_head = route((stale_w3[0], stale_w1[0], stale_head[0]), swap_weights)
    teach_hidden = grouped_pre(group_taps, teach_w3)[1]
    teacher_part = teacher_tail(images, teach_hidden, teach_w1, teach_head)
    logits, teacher = sum_logits(student_part, teacher_part)
    onehot = (labels[:, None] == jnp.arange(K, dtype=jnp.int32)[None, :]).astype(jnp.float32)
    dlogit = 2.0 * jax.nn.softmax(logits, axis=-1) - onehot - jax.nn.softmax(teacher, axis=-1)
    grad_head = jnp.dot(pooled, dlogit, precision=lax.Precision.HIGHEST)
    dpooled = jnp.dot(dlogit, own_head.astype(jnp.float32).T, precision=lax.Precision.HIGHEST)
    dz_full = (
        dpooled.T[:, :, None]
        / (ROWS * MAP_W)
        * dsilu(z_mixed.reshape(local_chans, images.shape[1], images.shape[2]))
    )
    dz_half = dz_full.reshape(local_chans, columns_count).astype(jnp.bfloat16)
    grad_w1 = lax.dot_general(
        dz_half, full_hidden, (((1,), (1,)), ((), ())), preferred_element_type=jnp.float32
    )
    dhidden = lax.psum_scatter(
        lax.dot_general(
            own_w1, dz_half, (((0,), (0,)), ((), ())), preferred_element_type=jnp.float32
        ),
        "filt",
        scatter_dimension=0,
        tiled=True,
    )
    dpre = (dhidden * dsilu(pre)).astype(jnp.bfloat16)
    pieces = []
    for group in range(groups):
        part_grad = lax.dot_general(
            dpre[group::groups],
            group_taps[group],
            (((1,), (1,)), ((), ())),
            preferred_element_type=jnp.float32,
        )
        pieces.append(part_grad.reshape(local_chans // groups, 9, GW))
    grad_w3 = jnp.stack(pieces, axis=1).reshape(local_chans, 9, GW)
    return (grad_w3[None], grad_w1[None], grad_head[None])


def solution(mesh):
    in_specs = (
        P("filt", "rep", None),
        P("rep"),
        P(),
        P("rep", "filt", None, None),
        P("rep", "filt", None),
        P("rep", "filt", None),
        P("rep", "filt", None, None),
        P("rep", "filt", None),
        P("rep", "filt", None),
    )
    out_specs = (P("rep", "filt", None, None), P("rep", "filt", None), P("rep", "filt", None))
    return jax.shard_map(
        per_device, mesh=mesh, in_specs=in_specs, out_specs=out_specs, check_vma=False
    )
```

profile of v0, /device:TPU:1, one launch (start us, length us, event | category | flops | bytes accessed | tf_op | source)
XLA Modules:
  0.0 711.5 jit_solution(7969254479247259533)
XLA Ops:
  7.2 2.6 collective-permute-start.4
  9.9 1.4 collective-permute-start.8
  11.3 4.4 copy.69
  17.1 95.3 %all_gather.9 = bf16[2016,1,224]{2,1,0:T(2,128)(2,1)S(1)} all-gather(bf16[126,1,224]{2,1,0:T(2,128)(2,1)S(1)} %copy.61), channel_id=1, replica_groups=mesh['rep'=16,'filt'=16] {'filt'}, dimensions={0}, use_global_device_ids=true | all-gather | bytes 959616 | tf_op jit(solution)/shard_map/all_gather | solution.py:106
  112.3 2.9 fusion.28
  115.3 1.2 copy.97
  116.5 4.4 copy.71
  120.9 1.9 bitcast_select_fusion
  122.8 2.6 copy.72
  125.4 4.8 collective-permute-start.5
  130.2 2.0 pad_slice_fusion.8
  132.2 4.4 copy.63
  136.5 10.6 %slice.83 = bf16[63,9,1008]{2,0,1:T(8,128)(2,1)} slice(bf16[126,9,1008]{2,0,1:T(8,128)(2,1)} %bitcast.127), slice={[0:126:2], [0:9:1], [0:1008:1]} | slice | bytes 2286144 | tf_op jit(solution)/shard_map/slice | solution.py:52
  147.2 10.6 %slice.93 = bf16[63,9,1008]{2,0,1:T(8,128)(2,1)} slice(bf16[126,9,1008]{2,0,1:T(8,128)(2,1)} %bitcast.128), slice={[1:126:2], [0:9:1], [0:1008:1]} | slice | bytes 2286144 | tf_op jit(solution)/shard_map/slice | solution.py:52
  157.8 3.5 copy.98
  161.2 1.9 constant_dynamic-update-slice_fusion.7
  163.2 4.2 pad_slice_fusion
  177.8 53.1 %collective-permute-done.5 = bf16[126,9,1008]{0,2,1:T(8,128)(2,1)} collective-permute-done((bf16[126,9,1008]{0,2,1:T(8,128)(2,1)}, bf16[126,9,1008]{0,2,1:T(8,128)(2,1)}, u32[]{:S(2)}, u32[]{:S(2)}) %collective-permute-start.5) | collective-permute-done | bytes 2286176 | tf_op jit(solution)/shard_map/ppermute | solution.py:20
  231.0 4.4 copy.73
  235.3 3.5 broadcast_select_fusion
  238.8 4.6 copy.74
  243.4 1.2 collective-permute-start.6
  247.8 3.6 convolution_bitcast_fusion.8
  251.4 3.6 convolution_bitcast_fusion.7
  256.9 2.4 collective-permute-start.1
  259.4 35.6 %collective-permute-done.6 = bf16[126,9,1008]{0,2,1:T(8,128)(2,1)} collective-permute-done((bf16[126,9,1008]{0,2,1:T(8,128)(2,1)}, bf16[126,9,1008]{0,2,1:T(8,128)(2,1)}, u32[]{:S(2)}, u32[]{:S(2)}) %collective-permute-start.6) | collective-permute-done | bytes 2286176 | tf_op jit(solution)/shard_map/ppermute | solution.py:20
  295.0 4.4 copy.75
  299.4 1.9 broadcast_select_fusion.1
  301.3 2.6 copy.76
  303.9 2.7 collective-permute-start.7
  306.6 29.7 %all-gather = bf16[16,126,224]{1,2,0:T(8,128)(2,1)S(1)} all-gather(bf16[1,126,224]{1,2,0:T(8,128)(2,1)} %fusion.17), channel_id=1, replica_groups=mesh['rep'=16,'filt'=16] {'filt'}, dimensions={0}, use_global_device_ids=true | all-gather | bytes 959616 | tf_op jit(solution)/shard_map/all_gather | solution.py:109
  336.3 1.3 copy.68
  337.6 2.8 reshape.130
  340.4 1.7 broadcast_select_fusion.7
  342.4 1.9 broadcast_select_fusion.4
  344.3 1.2 collective-permute-start.2
  345.5 1.6 multiply_reduce_fusion.1
  347.7 1.3 fusion.7
  349.0 12.6 %collective-permute-done.10 = bf16[126,1000]{0,1:T(8,128)(2,1)} collective-permute-done((bf16[126,1000]{0,1:T(8,128)(2,1)}, bf16[126,1000]{0,1:T(8,128)(2,1)}, u32[]{:S(2)}, u32[]{:S(2)}) %collective-permute-start.10) | collective-permute-done | bytes 252032 | tf_op jit(solution)/shard_map/ppermute | solution.py:20
  362.6 1.8 collective-permute-start.11
  364.5 8.2 %collective-permute-done.2 = bf16[126,2016]{0,1:T(8,128)(2,1)} collective-permute-done((bf16[126,2016]{0,1:T(8,128)(2,1)}, bf16[126,2016]{0,1:T(8,128)(2,1)}, u32[]{:S(2)}, u32[]{:S(2)}) %collective-permute-start.2) | collective-permute-done | bytes 508064 | tf_op jit(solution)/shard_map/ppermute | solution.py:20
  372.7 1.9 broadcast_select_fusion.5
  374.6 1.7 collective-permute-start.3
  376.3 4.4 copy.77
  380.7 3.5 broadcast_select_fusion.2
  384.3 8.9 %slice.94 = bf16[63,9,1008]{2,0,1:T(8,128)(2,1)S(1)} slice(bf16[126,9,1008]{2,0,1:T(8,128)(2,1)} %broadcast_select_fusion.2), slice={[0:126:2], [0:9:1], [0:1008:1]} | slice | bytes 2286144 | tf_op jit(solution)/shard_map/slice | solution.py:52
  393.2 8.9 %slice.95 = bf16[63,9,1008]{2,0,1:T(8,128)(2,1)S(1)} slice(bf16[126,9,1008]{2,0,1:T(8,128)(2,1)} %broadcast_select_fusion.2), slice={[1:126:2], [0:9:1], [0:1008:1]} | slice | bytes 2286144 | tf_op jit(solution)/shard_map/slice | solution.py:52
  402.1 3.6 convolution_bitcast_fusion.6
  405.6 3.6 convolution_bitcast_fusion.5
  409.6 31.6 %all-gather.1 = bf16[16,126,224]{1,2,0:T(8,128)(2,1)S(1)} all-gather(bf16[1,126,224]{1,2,0:T(8,128)(2,1)S(1)} %fusion.18), channel_id=1, replica_groups=mesh['rep'=16,'filt'=16] {'filt'}, dimensions={0}, use_global_device_ids=true | all-gather | bytes 959616 | tf_op jit(solution)/shard_map/all_gather | solution.py:72
  441.5 2.2 reshape.132
  443.8 1.9 multiply_reduce_fusion
  445.6 1.3 fusion.9
  447.0 43.0 %all-reduce.3 = (f32[1,1000]{1,0:T(1,128)S(1)}, f32[1,1000]{1,0:T(1,128)S(1)}) all-reduce(f32[1,1000]{1,0:T(1,128)S(1)} %fusion.9, f32[1,1000]{1,0:T(1,128)S(1)} %fusion.7), channel_id=1, replica_groups=mesh['rep'=16,'filt'=16] {'filt'}, use_global_device_ids=true, to_apply=%region_5.6 | all-reduce | flops 2000 | bytes 16000 | tf_op jit(solution)/shard_map/psum | solution.py:79
  491.2 2.0 fusion.26
  493.1 2.6 divide_subtract_fusion
  496.0 1.8 convolution_bitcast_fusion
  499.6 2.2 copy.87
  502.8 176.1 %all-reduce.6.cloned.1.call-done = f32[2016,224]{0,1:T(8,128)} async-done(((f32[2016,224]{0,1:T(8,128)}), f32[2016,224]{0,1:T(8,128)}) %all-reduce.6.cloned.1.call-update) | async-done | bytes 1806352
  678.9 1.0 fusion.12
  682.0 3.1 convolution_bitcast_fusion.3
  685.0 3.1 convolution_bitcast_fusion.2
  688.7 6.1 copy.93
  694.8 9.9 %reshape.145 = f32[1,126,9,1008]{3,0,2,1:T(1,128)} reshape(f32[63,2,9,1008]{3,2,1,0:T(8,128)} %copy.93) | data formatting | bytes 9144576
  (102 shorter events, 24.7 us)
Async XLA Ops:
  7.2 338.3 %copy-start = (bf16[1,126,2016]{1,2,0:T(8,128)(2,1)S(1)}, bf16[1,126,2016]{1,2,0:T(8,128)(2,1)}, u32[]{:S(2)}) copy-start(bf16[1,126,2016]{1,2,0:T(8,128)(2,1)} %param.13) | copy-start | bytes 1524100
  7.2 8.5 %copy-start.21 = (s32[16]{0:T(128)S(1)}, s32[16]{0:T(128)}, u32[]{:S(2)}) copy-start(s32[16]{0:T(128)} %param.11) | copy-start | bytes 196
  7.2 9.7 %copy-start.19 = (bf16[126,1,224]{0,2,1:T(8,128)(2,1)S(1)}, bf16[126,1,224]{0,2,1:T(8,128)(2,1)}, u32[]{:S(2)}) copy-start(bf16[126,1,224]{0,2,1:T(8,128)(2,1)} %param.9) | copy-start | bytes 169348
  7.2 671.7 %all-reduce.6.cloned.1.call-start = ((), (), s32[]{:S(2)}) async-start(), calls=%async_computation | async-start | bytes 3670016
  7.2 109.3 %collective-permute-start.4 = (bf16[126,9,1008]{0,2,1:T(8,128)(2,1)}, bf16[126,9,1008]{0,2,1:T(8,128)(2,1)}, u32[]{:S(2)}, u32[]{:S(2)}) collective-permute-start(bf16[126,9,1008]{0,2,1:T(8,128)(2,1)} %bitcast.131), channel_id=1, source_target_pairs={{0,16},{16,0},{32,48},{48,32},{64,80},{80,64},{96,112},{112,96},{1... | collective-permute-start | bytes 6858440 | tf_op jit(solution)/shard_map/ppermute | solution.py:20
  9.8 247.0 %collective-permute-start = (bf16[126,2016]{0,1:T(8,128)(2,1)}, bf16[126,2016]{0,1:T(8,128)(2,1)}, u32[]{:S(2)}, u32[]{:S(2)}) collective-permute-start(bf16[126,2016]{0,1:T(8,128)(2,1)} %bitcast.148), channel_id=1, source_target_pairs={{0,16},{16,0},{32,48},{48,32},{64,80},{80,64},{96,112},{112,96},{1... | collective-permute-start | bytes 1524104 | tf_op jit(solution)/shard_map/ppermute | solution.py:20
  9.9 246.2 %collective-permute-start.8 = (bf16[126,1000]{0,1:T(8,128)(2,1)}, bf16[126,1000]{0,1:T(8,128)(2,1)}, u32[]{:S(2)}, u32[]{:S(2)}) collective-permute-start(bf16[126,1000]{0,1:T(8,128)(2,1)} %bitcast.149), channel_id=1, source_target_pairs={{0,16},{16,0},{32,48},{48,32},{64,80},{80,64},{96,112},{112,96},{1... | collective-permute-start | bytes 756008 | tf_op jit(solution)/shard_map/ppermute | solution.py:20
  125.4 105.6 %collective-permute-start.5 = (bf16[126,9,1008]{0,2,1:T(8,128)(2,1)}, bf16[126,9,1008]{0,2,1:T(8,128)(2,1)}, u32[]{:S(2)}, u32[]{:S(2)}) collective-permute-start(bf16[126,9,1008]{0,2,1:T(8,128)(2,1)} %copy.72), channel_id=1, source_target_pairs={{0,32},{32,0},{16,48},{48,16},{64,96},{96,64},{80,112},{112,80},{1... | collective-permute-start | bytes 6858440 | tf_op jit(solution)/shard_map/ppermute | solution.py:20
  161.2 6.9 copy-start.15
  161.2 7.7 %copy-start.14 = (bf16[1008,1,4,56]{0,3,2,1:T(8,128)(2,1)S(1)}, bf16[1008,1,4,56]{0,3,2,1:T(8,128)(2,1)}, u32[]{:S(2)}) copy-start(bf16[1008,1,4,56]{0,3,2,1:T(8,128)(2,1)} %get-tuple-element.21) | copy-start | bytes 1354756
  161.2 8.5 %copy-start.13 = (bf16[1008,1,4,56]{0,3,2,1:T(8,128)(2,1)S(1)}, bf16[1008,1,4,56]{0,3,2,1:T(8,128)(2,1)}, u32[]{:S(2)}) copy-start(bf16[1008,1,4,56]{0,3,2,1:T(8,128)(2,1)} %get-tuple-element.22) | copy-start | bytes 1354756
  163.2 8.2 %copy-start.12 = (bf16[1008,1,4,56]{0,3,2,1:T(8,128)(2,1)S(1)}, bf16[1008,1,4,56]{0,3,2,1:T(8,128)(2,1)}, u32[]{:S(2)}) copy-start(bf16[1008,1,4,56]{0,3,2,1:T(8,128)(2,1)} %get-tuple-element.23) | copy-start | bytes 1354756
  163.2 9.0 %copy-start.11 = (bf16[1008,1,4,56]{0,3,2,1:T(8,128)(2,1)S(1)}, bf16[1008,1,4,56]{0,3,2,1:T(8,128)(2,1)}, u32[]{:S(2)}) copy-start(bf16[1008,1,4,56]{0,3,2,1:T(8,128)(2,1)} %get-tuple-element.24) | copy-start | bytes 1354756
  167.3 5.7 copy-start.10
  167.3 6.5 copy-start.9
  169.8 7.2 %copy-start.3 = (bf16[1008,1,224]{0,2,1:T(8,128)(2,1)S(1)}, bf16[1008,1,224]{0,2,1:T(8,128)(2,1)}, u32[]{:S(2)}) copy-start(bf16[1008,1,224]{0,2,1:T(8,128)(2,1)} %copy.98) | copy-start | bytes 1354756
  235.3 9.3 %copy-start.8 = (bf16[1008,1,4,56]{0,3,2,1:T(8,128)(2,1)S(1)}, bf16[1008,1,4,56]{0,3,2,1:T(8,128)(2,1)}, u32[]{:S(2)}) copy-start(bf16[1008,1,4,56]{0,3,2,1:T(8,128)(2,1)} %get-tuple-element.31) | copy-start | bytes 1354756
  238.8 6.6 copy-start.7
  238.8 7.4 %copy-start.6 = (bf16[1008,1,4,56]{0,3,2,1:T(8,128)(2,1)S(1)}, bf16[1008,1,4,56]{0,3,2,1:T(8,128)(2,1)}, u32[]{:S(2)}) copy-start(bf16[1008,1,4,56]{0,3,2,1:T(8,128)(2,1)} %get-tuple-element.33) | copy-start | bytes 1354756
  238.8 8.2 %copy-start.5 = (bf16[1008,1,4,56]{0,3,2,1:T(8,128)(2,1)S(1)}, bf16[1008,1,4,56]{0,3,2,1:T(8,128)(2,1)}, u32[]{:S(2)}) copy-start(bf16[1008,1,4,56]{0,3,2,1:T(8,128)(2,1)} %get-tuple-element.27) | copy-start | bytes 1354756
  238.8 9.0 %copy-start.2 = (bf16[63,9,1008]{2,0,1:T(8,128)(2,1)S(1)}, bf16[63,9,1008]{2,0,1:T(8,128)(2,1)}, u32[]{:S(2)}) copy-start(bf16[63,9,1008]{2,0,1:T(8,128)(2,1)} %slice.83) | copy-start | bytes 3429220
  243.4 51.6 %collective-permute-start.6 = (bf16[126,9,1008]{0,2,1:T(8,128)(2,1)}, bf16[126,9,1008]{0,2,1:T(8,128)(2,1)}, u32[]{:S(2)}, u32[]{:S(2)}) collective-permute-start(bf16[126,9,1008]{0,2,1:T(8,128)(2,1)} %copy.74), channel_id=1, source_target_pairs={{0,64},{64,0},{16,80},{80,16},{32,96},{96,32},{48,112},{112,48},{1... | collective-permute-start | bytes 6858440 | tf_op jit(solution)/shard_map/ppermute | solution.py:20
  246.2 5.2 copy-start.1
  251.4 4.7 copy-start.18
  251.4 5.4 copy-start.17
  256.8 83.5 %collective-permute-start.9 = (bf16[126,1000]{0,1:T(8,128)(2,1)}, bf16[126,1000]{0,1:T(8,128)(2,1)}, u32[]{:S(2)}, u32[]{:S(2)}) collective-permute-start(bf16[126,1000]{0,1:T(8,128)(2,1)} %broadcast_select_fusion.6), channel_id=1, source_target_pairs={{0,32},{32,0},{16,48},{48,16},{64,96},{96,64},{80,112},{112,80},{1... | collective-permute-start | bytes 756008 | tf_op jit(solution)/shard_map/ppermute | solution.py:20
  256.9 85.4 %collective-permute-start.1 = (bf16[126,2016]{0,1:T(8,128)(2,1)S(1)}, bf16[126,2016]{0,1:T(8,128)(2,1)}, u32[]{:S(2)}, u32[]{:S(2)}) collective-permute-start(bf16[126,2016]{0,1:T(8,128)(2,1)S(1)} %broadcast_select_fusion.3), channel_id=1, source_target_pairs={{0,32},{32,0},{16,48},{48,16},{64,96},{96,64},{80,112},{112,80},{1... | collective-permute-start | bytes 1524104 | tf_op jit(solution)/shard_map/ppermute | solution.py:20
  303.9 72.4 %collective-permute-start.7 = (bf16[126,9,1008]{0,2,1:T(8,128)(2,1)}, bf16[126,9,1008]{0,2,1:T(8,128)(2,1)}, u32[]{:S(2)}, u32[]{:S(2)}) collective-permute-start(bf16[126,9,1008]{0,2,1:T(8,128)(2,1)} %copy.76), channel_id=1, source_target_pairs={{0,128},{128,0},{16,144},{144,16},{32,160},{160,32},{48,176},{176,... | collective-permute-start | bytes 6858440 | tf_op jit(solution)/shard_map/ppermute | solution.py:20
  342.1 19.5 %collective-permute-start.10 = (bf16[126,1000]{0,1:T(8,128)(2,1)}, bf16[126,1000]{0,1:T(8,128)(2,1)}, u32[]{:S(2)}, u32[]{:S(2)}) collective-permute-start(bf16[126,1000]{0,1:T(8,128)(2,1)} %broadcast_select_fusion.7), channel_id=1, source_target_pairs={{0,64},{64,0},{16,80},{80,16},{32,96},{96,32},{48,112},{112,48},{1... | collective-permute-start | bytes 756008 | tf_op jit(solution)/shard_map/ppermute | solution.py:20
  344.3 28.4 %collective-permute-start.2 = (bf16[126,2016]{0,1:T(8,128)(2,1)}, bf16[126,2016]{0,1:T(8,128)(2,1)}, u32[]{:S(2)}, u32[]{:S(2)}) collective-permute-start(bf16[126,2016]{0,1:T(8,128)(2,1)} %broadcast_select_fusion.4), channel_id=1, source_target_pairs={{0,64},{64,0},{16,80},{80,16},{32,96},{96,32},{48,112},{112,48},{1... | collective-permute-start | bytes 1524104 | tf_op jit(solution)/shard_map/ppermute | solution.py:20
  362.6 83.0 %collective-permute-start.11 = (bf16[126,1000]{0,1:T(8,128)(2,1)S(1)}, bf16[126,1000]{0,1:T(8,128)(2,1)}, u32[]{:S(2)}, u32[]{:S(2)}) collective-permute-start(bf16[126,1000]{0,1:T(8,128)(2,1)S(1)} %broadcast_select_fusion.8), channel_id=1, source_target_pairs={{0,128},{128,0},{16,144},{144,16},{32,160},{160,32},{48,176},{176,... | collective-permute-start | bytes 756008 | tf_op jit(solution)/shard_map/ppermute | solution.py:20
  374.6 69.2 %collective-permute-start.3 = (bf16[126,2016]{0,1:T(8,128)(2,1)}, bf16[126,2016]{0,1:T(8,128)(2,1)}, u32[]{:S(2)}, u32[]{:S(2)}) collective-permute-start(bf16[126,2016]{0,1:T(8,128)(2,1)} %broadcast_select_fusion.5), channel_id=1, source_target_pairs={{0,128},{128,0},{16,144},{144,16},{32,160},{160,32},{48,176},{176,... | collective-permute-start | bytes 1524104 | tf_op jit(solution)/shard_map/ppermute | solution.py:20
  409.2 34.6 %copy-start.20 = (bf16[126,1,224]{0,2,1:T(8,128)(2,1)S(1)}, bf16[126,1,224]{0,2,1:T(8,128)(2,1)}, u32[]{:S(2)}) copy-start(bf16[126,1,224]{0,2,1:T(8,128)(2,1)} %param.9) | copy-start | bytes 169348
  409.4 86.3 %copy-start.16 = (bf16[1,126,1000]{1,2,0:T(8,128)(2,1)S(1)}, bf16[1,126,1000]{1,2,0:T(8,128)(2,1)}, u32[]{:S(2)}) copy-start(bf16[1,126,1000]{1,2,0:T(8,128)(2,1)} %param.14) | copy-start | bytes 756004
  443.8 54.0 %copy-start.22 = (u32[256]{0:T(256)S(1)}, u32[256]{0:T(256)}, u32[]{:S(2)}) copy-start(u32[256]{0:T(256)} %constant.55) | copy-start | bytes 3076
  443.8 55.2 %copy-start.4 = (bf16[2016,224]{0,1:T(8,128)(2,1)S(1)}, bf16[2016,224]{0,1:T(8,128)(2,1)}, u32[]{:S(2)}) copy-start(bf16[2016,224]{0,1:T(8,128)(2,1)} %reshape.130) | copy-start | bytes 2709508
Sparse Core Ops, SparseCore 0:
  497.9 180.9 all-reduce.5
where the time goes:
time: 714 us; the launch traced here: 712 us
  waiting for transfers between devices  286 us (40%)
  blocking collectives  199 us (28%)
  local copies, waits for them, and re-layouts  133 us (19%)
  matrix products  29.1 us (4%)
  other arithmetic  27.4 us (4%)
  starting transfers between devices  20.2 us (3%)
  between operations  16.3 us (2%)
    unnamed x2, waiting for transfers between devices  176 us
    ppermute x12, waiting for transfers between devices, swapped(): return lax.ppermute(block, axis, route)  110 us
    all_gather x1, blocking collectives, per_device(): full_panel = lax.all_gather(images, 'filt', axis=0, tiled=True)  95.3 us
    unnamed x73, local copies, waits for them, and re-layouts  51.4 us
    psum x1, blocking collectives, sum_logits(): return lax.psum((student_part, teacher_part), 'filt')  43 us
    slice x4, local copies, waits for them, and re-layouts, grouped_pre(): weights = conv_w3[group::groups].reshape(local_chans // groups, 9 * GW)  39 us
    all_gather x1, blocking collectives, teacher_tail(): lax.all_gather(hidden, 'filt', axis=0, tiled=True)  31.6 us
    all_gather x1, blocking collectives, per_device(): full_hidden = lax.all_gather(hidden, 'filt', axis=0, tiled=True)  29.7 us
  transfers between devices with their start and end apart: 13, of which 5 were waited for; matrix products, arithmetic and copies ran while one was open for 22% of the time, Pallas kernels for 0%

commit v1 on v0

v1 whole, which is shorter than its diff:
```python
import functools

import jax
import jax.numpy as jnp
from jax import lax
from jax.experimental import pallas as pl
from jax.experimental.pallas import tpu as pltpu
from jax.sharding import PartitionSpec as P

C = 2016
GW = 1008
K = 1000
ROWS = 4
MAP_W = 56
POS = ROWS * MAP_W
N_REP = 16
N_FILT = 16
LOC = C // N_FILT
HALF = LOC // 2
RELAY = 32
CHUNKS = POS // RELAY
LANES = 128
F32 = jnp.float32
BF16 = jnp.bfloat16
MESH = pl.DeviceIdType.MESH


def mm(a, b, dims=((1,), (0,))):
    return lax.dot_general(a, b, (dims, ((), ())), preferred_element_type=F32)


def silu(v):
    return v / (1.0 + jnp.exp(-v))


def dsilu(v):
    sig = 1.0 / (1.0 + jnp.exp(-v))
    return sig * (1.0 + v * (1.0 - sig))


def split3(v):
    hi = v.astype(BF16)
    rest = v - hi.astype(F32)
    mid = rest.astype(BF16)
    low = (rest - mid.astype(F32)).astype(BF16)
    pad = jnp.zeros((13,) + v.shape[1:], BF16)
    return jnp.concatenate([hi, mid, low, pad], axis=0)


class Gather:
    def __init__(self, panel, send, recv, here):
        self.panel, self.send, self.recv, self.here = panel, send, recv, here
        self.started = []

    def copy(self, kind, slot, target):
        where = self.panel.at[:, pl.ds(pl.multiple_of(slot * LANES, LANES), LANES)]
        return pltpu.make_async_remote_copy(
            src_ref=where,
            dst_ref=where,
            send_sem=self.send.at[kind],
            recv_sem=self.recv.at[kind],
            device_id={"rep": self.here.rep, "filt": target},
            device_id_type=MESH,
        )

    def go(self, kind, slot, target):
        made = self.copy(kind, slot, target)
        made.start()
        self.started.append(made)

    def got(self, kind, slot):
        self.copy(kind, slot, self.here.sib).wait_recv()

    def own(self):
        h = self.here
        self.go(0, h.me, h.opp)
        self.go(1, h.me, h.right)
        self.go(2, h.me, h.left)
        self.go(7, h.me, h.sib)

    def across(self):
        h = self.here
        self.got(0, h.opp)
        self.go(3, h.opp, h.right)
        self.go(4, h.opp, h.left)
        self.go(8, h.opp, h.sib)

    def near(self):
        h = self.here
        self.got(1, h.left)
        self.go(5, h.left, h.right)
        self.go(9, h.left, h.sib)
        self.got(2, h.right)
        self.go(10, h.right, h.sib)

    def near_opp(self):
        h = self.here
        self.got(4, h.right_opp)
        self.go(6, h.right_opp, h.left)
        self.go(11, h.right_opp, h.sib)
        self.got(3, h.left_opp)
        self.go(12, h.left_opp, h.sib)

    def far(self):
        h = self.here
        self.got(5, h.far)
        self.go(13, h.far, h.sib)

    def far_opp(self):
        h = self.here
        self.got(6, h.far_opp)
        self.go(14, h.far_opp, h.sib)

    def plane(self):
        h = self.here
        self.got(7, h.sib)
        self.got(9, h.other(h.left))
        self.got(10, h.other(h.right))
        self.got(13, h.other(h.far))

    def plane_opp(self):
        h = self.here
        self.got(8, h.other(h.opp))
        self.got(11, h.other(h.right_opp))
        self.got(12, h.other(h.left_opp))
        self.got(14, h.other(h.far_opp))

    def drain(self):
        for made in self.started:
            made.wait_send()


class Here:
    def __init__(self):
        self.rep = lax.axis_index("rep")
        self.me = lax.axis_index("filt")
        self.z = self.me // 8
        self.y = (self.me % 8) // 2
        self.k = self.me % 2
        self.up = (self.y + 1) % 4
        self.down = (self.y + 3) % 4
        self.beyond = (self.y + 2) % 4
        self.sib = self.at(self.z, self.y, 1 - self.k)
        self.opp = self.at(1 - self.z, self.y, self.k)
        self.right = self.at(self.z, self.up, self.k)
        self.left = self.at(self.z, self.down, self.k)
        self.far = self.at(self.z, self.beyond, self.k)
        self.right_opp = self.at(1 - self.z, self.up, self.k)
        self.left_opp = self.at(1 - self.z, self.down, self.k)
        self.far_opp = self.at(1 - self.z, self.beyond, self.k)

    def at(self, z, y, k):
        return z * 8 + y * 2 + k

    def other(self, slot):
        return slot + 1 - 2 * (slot % 2)


def main_kernel(
    label, partner_h, x_h, w3s_h, w1s_h, hds_h, w3t_h, w1t_h, hdt_h,
    xeo, hc, dz_out, dpre_out, dl_out, pooled_out,
    partner, x, w3s, w3t, wxs, wxt, w1raw, w1p, hds, hdt, xg, xgt, hg, hgt, accs, acct,
    a1, sb, ls, lt, ua, row, sendb, block, ra, rb, rc,
    wsem, gsend, grecv, asend, arecv, lsend, lrecv, rsend, rrecv,
):
    h = Here()
    rep, me = h.rep, h.me

    barrier = pltpu.get_barrier_semaphore()
    for i in range(1, N_REP):
        pl.semaphore_signal(
            barrier, inc=1, device_id={"rep": (rep + i) % N_REP, "filt": me}, device_id_type=MESH
        )
    for i in range(1, N_FILT):
        pl.semaphore_signal(
            barrier, inc=1, device_id={"rep": rep, "filt": (me + i) % N_FILT}, device_id_type=MESH
        )

    loads = [
        pltpu.make_async_copy(src, dst, wsem.at[i])
        for i, (src, dst) in enumerate(
            (
                (x_h, x),
                (partner_h, partner),
                (w3s_h, w3s),
                (w3t_h, w3t),
                (w1s_h, w1raw.at[0]),
                (w1t_h, w1raw.at[1]),
                (hds_h, hds),
                (hdt_h, hdt),
            )
        )
    ]
    for load in loads:
        load.start()

    lane_from = lax.broadcasted_iota(jnp.int32, (LOC, LANES), 0)
    lane_to = lax.broadcasted_iota(jnp.int32, (LOC, LANES), 1)
    inside = lane_to % 64
    perm = jnp.where((inside < HALF) & (lane_from == 2 * inside + lane_to // 64), 1.0, 0.0)
    perm = perm.astype(BF16)
    own = pl.ds(pl.multiple_of(me * LANES, LANES), LANES)
    loads[0].wait()
    xg[:, own] = mm(x[...], perm).astype(BF16)

    pl.semaphore_wait(barrier, N_REP - 1 + N_FILT - 1)

    gx = Gather(xg, gsend.at[0], grecv.at[0], h)
    gxt = Gather(xgt, gsend.at[1], grecv.at[1], h)
    gh = Gather(hg, gsend.at[2], grecv.at[2], h)
    ght = Gather(hgt, gsend.at[3], grecv.at[3], h)

    for i in range(1, N_REP):
        q = (rep + i) % N_REP

        @pl.when(q < CHUNKS)
        def _():
            pltpu.make_async_remote_copy(
                src_ref=xg.at[pl.ds(pl.multiple_of(q * RELAY, RELAY), RELAY), own],
                dst_ref=a1.at[rep],
                send_sem=asend.at[0],
                recv_sem=arecv.at[0],
                device_id={"rep": q, "filt": me},
                device_id_type=MESH,
            ).start()

    gx.own()
    loads[1].wait()

    def ordered(w3, wx, first, last):
        keep = lax.broadcasted_iota(jnp.int32, (64, LOC), 0) < HALF
        even = lax.broadcasted_iota(jnp.int32, (64, LOC), 1) % 2 == 0

        def body(t, carry):
            where = pl.ds(pl.multiple_of(t * LANES, LANES), LOC)
            w = jnp.concatenate([w3[t].astype(F32), jnp.zeros((8, LOC), F32)], axis=0)
            for f in range(N_FILT):
                piece = w[f * HALF : f * HALF + 64]
                wx[f * LANES : f * LANES + 64, where] = jnp.where(
                    keep & even, piece, 0.0
                ).astype(BF16)
                wx[f * LANES + 64 : (f + 1) * LANES, where] = jnp.where(
                    keep & ~even, piece, 0.0
                ).astype(BF16)
            return carry

        lax.fori_loop(first, last, body, 0)

    chunk = pl.ds(pl.multiple_of(rep * RELAY, RELAY), RELAY)
    loads[2].wait()
    ordered(w3s, wxs, 0, 3)

    @pl.when(rep < CHUNKS)
    def _():
        pltpu.make_async_copy(a1.at[pl.ds(0, 15)], a1.at[pl.ds(0, 15)], arecv.at[0]).wait()
        a1[rep] = xg[chunk, own]
        xgt[chunk, own] = a1[partner[rep]]
        for i in range(1, N_REP):
            p = (rep + i) % N_REP
            sb[i] = a1[partner[p]]
            pltpu.make_async_remote_copy(
                src_ref=sb.at[i],
                dst_ref=xgt.at[chunk, own],
                send_sem=asend.at[1],
                recv_sem=arecv.at[1],
                device_id={"rep": p, "filt": me},
                device_id_type=MESH,
            ).start()

    gx.near()
    ordered(w3s, wxs, 3, 6)
    gx.far()
    gx.across()

    @pl.when(rep < CHUNKS)
    def _():
        pltpu.make_async_copy(
            xgt.at[pl.ds(0, RELAY * (CHUNKS - 1)), own],
            xgt.at[pl.ds(0, RELAY * (CHUNKS - 1)), own],
            arecv.at[1],
        ).wait()

    @pl.when(rep >= CHUNKS)
    def _():
        pltpu.make_async_copy(xgt.at[:, own], xgt.at[:, own], arecv.at[1]).wait()

    gxt.own()
    ordered(w3s, wxs, 6, 9)
    gx.near_opp()
    gx.far_opp()

    def conv_half(panel, wx, acc, z, first):
        rows = pl.ds(pl.multiple_of(z * (8 * LANES), 8 * LANES), 8 * LANES)
        for i in range(3):
            where = slice(i * 3 * LANES, (i + 1) * 3 * LANES)
            part = mm(panel[:, rows], wx[rows, where])
            acc[:, where] = part if first else acc[:, where] + part

    lanes = lax.broadcasted_iota(jnp.int32, (POS, LANES), 1)
    column = lax.broadcasted_iota(jnp.int32, (POS, LANES), 0) % MAP_W

    def conv_end(acc):
        total = None
        top = jnp.zeros((MAP_W, LANES), F32)

        def tap(t, low, high):
            return acc[low:high, t * LANES : (t + 1) * LANES]

        for b in range(3):
            part = tap(3 + b, 0, POS)
            part = part + jnp.concatenate([top, tap(b, 0, POS - MAP_W)], axis=0)
            part = part + jnp.concatenate([tap(6 + b, MAP_W, POS), top], axis=0)
            if b == 0:
                part = jnp.where(column >= 1, pltpu.roll(part, 1, 0), 0.0)
            if b == 2:
                part = jnp.where(column <= MAP_W - 2, pltpu.roll(part, POS - 1, 0), 0.0)
            total = part if total is None else total + part
        return total

    def hidden_of(pre):
        return jnp.where(lanes < LOC, silu(pre), 0.0).astype(BF16)

    gxt.near()
    gx.plane()
    conv_half(xg, wxs, accs, h.z, True)
    gxt.far()
    gxt.across()
    gx.plane_opp()
    conv_half(xg, wxs, accs, 1 - h.z, False)
    pre = conv_end(accs)
    hg[:, own] = hidden_of(pre)
    gh.own()
    gxt.near_opp()
    loads[3].wait()
    ordered(w3t, wxt, 0, 4)
    gxt.far_opp()
    ordered(w3t, wxt, 4, 9)
    gh.near()
    gxt.plane()
    conv_half(xgt, wxt, acct, h.z, True)
    gh.far()
    gxt.plane_opp()
    conv_half(xgt, wxt, acct, 1 - h.z, False)
    hgt[:, own] = hidden_of(conv_end(acct))
    ght.own()
    gh.across()

    for which in range(2):
        loads[4 + which].wait()
        for f in range(N_FILT):
            w1p[which, f * LANES : f * LANES + LOC, :] = w1raw[which, f * LOC : (f + 1) * LOC, :]
            w1p[which, f * LANES + LOC : (f + 1) * LANES, :] = jnp.zeros((LANES - LOC, LOC), BF16)

    gh.near_opp()
    ght.near()
    gh.far_opp()
    ght.far()
    ght.across()
    gh.plane()
    gh.plane_opp()

    def logits_of(z, head):
        pooled = jnp.sum(silu(z), axis=0, keepdims=True) * (1.0 / POS)
        parts = mm(split3(pooled), head[...], ((1,), (1,)))
        row[...] = jnp.zeros((1, 1024), F32)
        row[:, :K] = parts[0:1] + parts[1:2] + parts[2:3]
        full = row[...]
        return pooled, jnp.concatenate(
            [full[:, i * LANES : (i + 1) * LANES] for i in range(8)], axis=0
        )

    def give_logits(buf, part, idx):
        buf[me] = part
        for i in range(1, N_FILT):
            pltpu.make_async_remote_copy(
                src_ref=buf.at[me],
                dst_ref=buf.at[me],
                send_sem=lsend.at[idx],
                recv_sem=lrecv.at[idx],
                device_id={"rep": rep, "filt": (me + i) % N_FILT},
                device_id_type=MESH,
            ).start()

    def wait_bytes(buf, count, sem):
        pltpu.make_async_copy(buf.at[pl.ds(0, count)], buf.at[pl.ds(0, count)], sem).wait()

    def sum_logits(buf, idx):
        wait_bytes(buf, N_FILT - 1, lrecv.at[idx])
        return jnp.sum(buf[...], axis=0)

    loads[6].wait()
    loads[7].wait()
    z_mixed = x[...].astype(F32) + mm(hg[...], w1p[0])
    pooled, part = logits_of(z_mixed, hds)
    give_logits(ls, part, 0)
    ght.near_opp()
    ght.far_opp()
    xt = mm(xgt[:, own], perm, ((1,), (1,)))
    ght.plane()
    ght.plane_opp()
    part = logits_of(xt + mm(hgt[...], w1p[1]), hdt)[1]
    give_logits(lt, part, 1)
    for f in range(N_FILT):
        hc[:, f * LOC : (f + 1) * LOC] = hg[:, f * LANES : f * LANES + LOC]
    logits = sum_logits(ls, 0)

    cls = lax.broadcasted_iota(jnp.int32, (8, LANES), 0) * LANES + lax.broadcasted_iota(
        jnp.int32, (8, LANES), 1
    )
    real = cls < K

    def softmax(v):
        top = jnp.max(jnp.where(real, v, -jnp.inf))
        e = jnp.where(real, jnp.exp(v - top), 0.0)
        return e / jnp.sum(e)

    own_part = 2.0 * softmax(logits) - jnp.where(cls == label[0], 1.0, 0.0)
    slope = dsilu(z_mixed) * (1.0 / POS)
    ua[rep] = sum_logits(lt, 1)
    for i in range(1, N_REP):
        pltpu.make_async_remote_copy(
            src_ref=ua.at[rep],
            dst_ref=ua.at[rep],
            send_sem=asend.at[2],
            recv_sem=arecv.at[2],
            device_id={"rep": (rep + i) % N_REP, "filt": me},
            device_id_type=MESH,
        ).start()
    pooled_out[...] = pooled
    for f in range(N_FILT):
        for g in range(2):
            xeo[g * POS : (g + 1) * POS, f * HALF : (f + 1) * HALF] = xg[
                :, f * LANES + 64 * g : f * LANES + 64 * g + HALF
            ]
    wait_bytes(ua, N_REP - 1, arecv.at[2])
    dl = own_part - softmax(ua[partner[rep]])
    dl_out[...] = dl
    dl_row = jnp.concatenate([dl[i : i + 1, :] for i in range(8)], axis=1)[:, :K]
    parts = mm(split3(dl_row), hds[...])
    dz = ((parts[0:1] + parts[1:2] + parts[2:3]) * slope).astype(BF16)
    dz_out[...] = dz

    def remote(src, dst, kind, target):
        return pltpu.make_async_remote_copy(
            src_ref=src,
            dst_ref=dst,
            send_sem=rsend.at[kind],
            recv_sem=rrecv.at[kind],
            device_id={"rep": rep, "filt": target},
            device_id_type=MESH,
        )

    targets = (
        h.at(0, h.beyond, h.k),
        h.at(1, h.beyond, h.k),
        h.at(0, h.up, h.k),
        h.at(1, h.down, h.k),
        h.at(1, h.up, h.k),
        h.at(0, h.down, h.k),
        h.opp,
        me,
    )
    mine_at = pl.ds(pl.multiple_of(h.k * LANES, LANES), LANES)
    other_at = pl.ds(pl.multiple_of((1 - h.k) * LANES, LANES), LANES)
    for z in range(2):
        rows = slice(z * 8 * LANES, (z + 1) * 8 * LANES)
        part = mm(dz, w1p[0, rows, :], ((1,), (1,)))
        for y in range(4):
            block[z * 4 + y] = part[:, y * 2 * LANES : (y + 1) * 2 * LANES]
    sib_copies = []
    for i, slot in enumerate(targets):
        sendb[i] = block[slot // 2, :, other_at].astype(BF16)
        made = remote(sendb.at[i], ra.at[i], i, h.sib)
        made.start()
        sib_copies.append(made)

    def chip_sum(i):
        sib_copies[i].wait_recv()
        return block[targets[i] // 2, :, mine_at] + ra[i].astype(F32)

    ring = []

    def ring_send(i, value, target):
        sendb[8 + i] = value.astype(BF16)
        made = remote(sendb.at[8 + i], rb.at[i], 8 + i, target)
        made.start()
        ring.append(made)

    ring_send(0, chip_sum(0), h.right)
    ring_send(1, chip_sum(1), h.left)
    ring_send(2, chip_sum(4), h.right)
    ring_send(3, chip_sum(5), h.left)
    up0 = chip_sum(2)
    down1 = chip_sum(3)
    ring[0].wait_recv()
    ring_send(4, up0 + rb[0].astype(F32), h.right)
    ring[1].wait_recv()
    ring_send(5, down1 + rb[1].astype(F32), h.left)
    to_opp = chip_sum(6)
    mine = chip_sum(7)
    ring[2].wait_recv()
    ring[3].wait_recv()
    ring[4].wait_recv()
    ring[5].wait_recv()
    low = h.z == 0
    sum0 = rb[4].astype(F32) + rb[3].astype(F32)
    sum1 = rb[5].astype(F32) + rb[2].astype(F32)
    sendb[14] = (to_opp + jnp.where(low, sum1, sum0)).astype(BF16)
    last = remote(sendb.at[14], rc, 14, h.opp)
    last.start()
    mine = mine + jnp.where(low, sum0, sum1)
    slope = dsilu(pre)
    last.wait_recv()
    dhidden = mine + rc[...].astype(F32)
    dpre_out[...] = (dhidden * slope)[:, :LOC].astype(BF16)

    for gather in (gx, gxt, gh, ght):
        gather.drain()
    for made in sib_copies + ring + [last]:
        made.wait_send()
    wait_bytes(ls, N_FILT - 1, lsend.at[0])
    wait_bytes(lt, N_FILT - 1, lsend.at[1])
    wait_bytes(ua, N_REP - 1, asend.at[2])

    @pl.when(rep < CHUNKS)
    def _():
        wait_bytes(sb, CHUNKS - 1, asend.at[0])
        wait_bytes(sb, N_REP - 1, asend.at[1])

    @pl.when(rep >= CHUNKS)
    def _():
        wait_bytes(sb, CHUNKS, asend.at[0])


def grads_kernel(xeo, hc, dz, dpre, dl, pooled, gw3, gw1, gh, turned, r3, r1, r0, sem):
    copies = []

    def out(src, dst, i):
        made = pltpu.make_async_copy(src, dst, sem.at[i])
        made.start()
        copies.append(made)

    dp = dpre[...].astype(F32)
    even = lax.broadcasted_iota(jnp.int32, (POS, LOC), 1) % 2 == 0
    column = lax.broadcasted_iota(jnp.int32, (POS, LOC), 0) % MAP_W
    zero = jnp.zeros((MAP_W, LOC), F32)
    for b in range(3):
        moved = dp
        if b == 0:
            moved = pltpu.roll(jnp.where(column >= 1, dp, 0.0), POS - 1, 0)
        if b == 2:
            moved = pltpu.roll(jnp.where(column <= MAP_W - 2, dp, 0.0), 1, 0)
        for a in range(3):
            d = moved
            if a == 0:
                d = jnp.concatenate([moved[MAP_W:], zero], axis=0)
            if a == 2:
                d = jnp.concatenate([zero, moved[: POS - MAP_W]], axis=0)
            where = slice(a * LANES, a * LANES + LOC)
            turned[b, :POS, where] = jnp.where(even, d, 0.0).astype(BF16)
            turned[b, POS:, where] = jnp.where(even, 0.0, d).astype(BF16)
    for b in range(3):
        rows = mm(turned[b], xeo[...], ((0,), (0,)))
        for a in range(3):
            t = 3 * a + b
            r3[t] = rows[a * LANES : a * LANES + LOC]
            out(r3.at[t], gw3.at[:, t, 0, :], t)
    r1[...] = mm(dz[...], hc[...], ((0,), (0,)))
    out(r1, gw1.at[:, 0, :], 9)
    flip = dl[...].T
    for i in range(8):
        size = min(LANES, K - i * LANES)
        r0[i * LANES : i * LANES + size, :] = flip[:size, i : i + 1] * pooled[...]
    out(r0, gh, 10)
    for made in copies:
        made.wait()


def per_device(
    images, labels, partner, student_w3, student_w1, student_head, stale_w3, stale_w1, stale_head
):
    vmem = pl.BlockSpec(memory_space=pltpu.VMEM)
    hbm = pl.BlockSpec(memory_space=pltpu.HBM)
    sds = jax.ShapeDtypeStruct
    dma = pltpu.SemaphoreType.DMA
    weights = []
    for w3, w1, head in (
        (student_w3, student_w1, student_head),
        (stale_w3, stale_w1, stale_head),
    ):
        weights += [w3[0].transpose(1, 2, 0), w1[0].T, head[0].T]
    saved = pl.pallas_call(
        main_kernel,
        out_shape=(
            pltpu.VMEM((2 * POS, GW), BF16),
            pltpu.VMEM((POS, C), BF16),
            pltpu.VMEM((POS, LOC), BF16),
            pltpu.VMEM((POS, LOC), BF16),
            pltpu.VMEM((8, LANES), F32),
            pltpu.VMEM((1, LOC), F32),
        ),
        in_specs=[pl.BlockSpec(memory_space=pltpu.SMEM)] + [hbm] * 8,
        out_specs=[vmem] * 6,
        scratch_shapes=[
            pltpu.SMEM((N_REP,), jnp.int32),
            pltpu.VMEM((POS, LOC), BF16),
            pltpu.VMEM((9, GW, LOC), BF16),
            pltpu.VMEM((9, GW, LOC), BF16),
            pltpu.VMEM((N_FILT * LANES, 9 * LANES), BF16),
            pltpu.VMEM((N_FILT * LANES, 9 * LANES), BF16),
            pltpu.VMEM((2, C, LOC), BF16),
            pltpu.VMEM((2, N_FILT * LANES, LOC), BF16),
            pltpu.VMEM((K, LOC), BF16),
            pltpu.VMEM((K, LOC), BF16),
            pltpu.VMEM((POS, N_FILT * LANES), BF16),
            pltpu.VMEM((POS, N_FILT * LANES), BF16),
            pltpu.VMEM((POS, N_FILT * LANES), BF16),
            pltpu.VMEM((POS, N_FILT * LANES), BF16),
            pltpu.VMEM((POS, 9 * LANES), F32),
            pltpu.VMEM((POS, 9 * LANES), F32),
            pltpu.VMEM((N_REP, RELAY, LANES), BF16),
            pltpu.VMEM((N_REP, RELAY, LANES), BF16),
            pltpu.VMEM((N_FILT, 8, LANES), F32),
            pltpu.VMEM((N_FILT, 8, LANES), F32),
            pltpu.VMEM((N_REP, 8, LANES), F32),
            pltpu.VMEM((1, 1024), F32),
            pltpu.VMEM((15, POS, LANES), BF16),
            pltpu.VMEM((8, POS, 2 * LANES), F32),
            pltpu.VMEM((8, POS, LANES), BF16),
            pltpu.VMEM((6, POS, LANES), BF16),
            pltpu.VMEM((POS, LANES), BF16),
            dma((8,)),
            dma((4, 15)),
            dma((4, 15)),
            dma((3,)),
            dma((3,)),
            dma((2,)),
            dma((2,)),
            dma((15,)),
            dma((15,)),
        ],
        compiler_params=pltpu.CompilerParams(
            collective_id=0, has_side_effects=True, vmem_limit_bytes=48 * 1024 * 1024
        ),
        name="step",
    )(
        labels,
        *(
            pltpu.with_memory_space_constraint(a, pltpu.HBM)
            for a in (partner, images.transpose(1, 2, 0)[0], *weights)
        ),
    )
    gw3, gw1, gh = pl.pallas_call(
        grads_kernel,
        out_shape=(
            sds((LOC, 9, 1, GW), F32),
            sds((LOC, 1, C), F32),
            sds((K, LOC), F32),
        ),
        in_specs=[vmem] * 6,
        out_specs=[hbm] * 3,
        scratch_shapes=[
            pltpu.VMEM((3, 2 * POS, 3 * LANES), BF16),
            pltpu.VMEM((9, LOC, GW), F32),
            pltpu.VMEM((LOC, C), F32),
            pltpu.VMEM((K, LOC), F32),
            dma((11,)),
        ],
        compiler_params=pltpu.CompilerParams(vmem_limit_bytes=40 * 1024 * 1024),
        name="grads",
    )(*saved)
    return (gw3.transpose(2, 0, 1, 3), gw1.transpose(1, 0, 2), gh.T[None])


def solution(mesh):
    in_specs = (
        P("filt", "rep", None),
        P("rep"),
        P(),
        P("rep", "filt", None, None),
        P("rep", "filt", None),
        P("rep", "filt", None),
        P("rep", "filt", None, None),
        P("rep", "filt", None),
        P("rep", "filt", None),
    )
    out_specs = (P("rep", "filt", None, None), P("rep", "filt", None), P("rep", "filt", None))
    return jax.shard_map(
        per_device, mesh=mesh, in_specs=in_specs, out_specs=out_specs, check_vma=False
    )
```

time: 714 us -> 92.7 us (0.13)
  waiting for transfers between devices: 286 us -> 0 us
  blocking collectives: 199 us -> 0 us
  local copies, waits for them, and re-layouts: 133 us -> 0 us
  Pallas kernels: 0 us -> 91.4 us
  matrix products: 29.1 us -> 0 us
  other arithmetic: 27.4 us -> 0 us
  starting transfers between devices: 20.2 us -> 0 us
  between operations: 16.3 us -> 1.29 us
    unnamed x2 -> x0, waiting for transfers between devices: 176 us -> none
    all_gather x3 -> x0, blocking collectives: 157 us -> none  [the longest x1 95.3 us: per_device(): full_panel = lax.all_gather(images, 'filt', axis=0, tiled=True)]
    ppermute x12 -> x0, waiting for transfers between devices: 110 us -> none  [swapped(): return lax.ppermute(block, axis, route)]
    pallas_call x0 -> x2, Pallas kernels: none -> 91.4 us  [the longest x1 87.7 us: per_device(): pl.pallas_call(main_kernel, out_shape=(pltpu.VMEM((2 * POS, GW), BF16), p...]
    unnamed x73 -> x0, local copies, waits for them, and re-layouts: 51.4 us -> none
    slice x9 -> x0, local copies, waits for them, and re-layouts: 50.1 us -> none  [the longest x4 39 us: grouped_pre(): weights = conv_w3[group::groups].reshape(local_chans // groups, 9 * GW)]
    psum x1 -> x0, blocking collectives: 43 us -> none  [sum_logits(): return lax.psum((student_part, teacher_part), 'filt')]
    dot_general x13 -> x0, matrix products: 29.1 us -> none  [the longest x4 14.3 us: grouped_pre(): jnp.dot(weights, group_taps[group], preferred_element_type=jnp.float32)]
  transfers between devices with their start and end apart: 13 -> 0, of which waited for: 5 -> 0; matrix products, arithmetic and copies ran while one was open for 22% -> 0% of each run, Pallas kernels for 0% -> 0%
where the time goes in v1:
time: 92.7 us; the launch traced here: 92.6 us
  Pallas kernels  91.4 us (99%)
  between operations  1.29 us (1%)
    pallas_call x1, Pallas kernels, per_device(): pl.pallas_call(main_kernel, out_shape=(pltpu.VMEM((2 * POS, GW), BF16), p...  87.7 us
    pallas_call x1, Pallas kernels, per_device(): pl.pallas_call(grads_kernel, out_shape=(sds((LOC, 9, 1, GW), F32), sds((L...  3.63 us

profile of v1, /device:TPU:1, one launch (start us, length us, event | category | flops | bytes accessed | tf_op | source)
XLA Modules:
  0.0 92.6 jit_solution(10148494701566412427)
XLA Ops:
  1.3 87.7 %step.1 = (bf16[448,1008]{1,0:T(8,128)(2,1)S(1)}, bf16[224,2016]{1,0:T(8,128)(2,1)S(1)}, bf16[224,126]{1,0:T(8,128)(2,1)S(1)}, bf16[224,126]{1,0:T(8,128)(2,1)S(...) custom-call(s32[1]{0:T(128)S(6)} %copy.12.label, s32[16]{0:T(128)} %partner_h.1, bf16[224,126]{1,0:T(8,128)(2,1)} %bitcast.32, ...), custom_call_target="tpu_custom_call" | custom-call | tf_op jit(solution)/shard_map/step/pallas_call | solution.py:592
  89.0 3.6 %grads.1 = (f32[126,9,1,1008]{3,2,1,0:T(1,128)}, f32[126,1,2016]{2,1,0:T(1,128)}, f32[1000,126]{1,0:T(8,128)}) custom-call(bf16[448,1008]{1,0:T(8,128)(2,1)S(1)} %get-tuple-element.12.xeo, bf16[224,2016]{1,0:T(8,128)(2,1)S(1)} %get-tuple-element.13.hc, bf16[224,126]{1,0:T(8,128)(2,1)S(1)} %get-tuple-element.14.dz, ...), custom_call_target="tpu_custom_call" | custom-call | tf_op jit(solution)/shard_map/grads/pallas_call | solution.py:653

commit v2 on v1

--- a/solution.py
+++ b/solution.py
@@ -48,12 +48,17 @@
 
 
 class Gather:
-    def __init__(self, panel, send, recv, here):
+    def __init__(self, panel, send, recv, here, parts=1):
         self.panel, self.send, self.recv, self.here = panel, send, recv, here
+        self.parts = parts
         self.started = []
 
-    def copy(self, kind, slot, target):
-        where = self.panel.at[:, pl.ds(pl.multiple_of(slot * LANES, LANES), LANES)]
+    def copy(self, kind, slot, target, part=None):
+        where = self.panel.at[slot]
+        if part is not None and self.parts > 1:
+            size = POS // self.parts
+            where = self.panel.at[slot, pl.ds(part * size, size)]
+            kind = kind if part == 0 else 15 + (0, 3, 4, 6).index(kind)
         return pltpu.make_async_remote_copy(
             src_ref=where,
             dst_ref=where,
@@ -63,53 +68,50 @@
             device_id_type=MESH,
         )
 
-    def go(self, kind, slot, target):
-        made = self.copy(kind, slot, target)
+    def go(self, kind, slot, target, part=None):
+        made = self.copy(kind, slot, target, part)
         made.start()
         self.started.append(made)
 
-    def got(self, kind, slot):
-        self.copy(kind, slot, self.here.sib).wait_recv()
+    def got(self, kind, slot, part=None):
+        self.copy(kind, slot, self.here.sib, part).wait_recv()
 
     def own(self):
+        for part in range(self.parts):
+            self.go(0, self.here.me, self.here.opp, part)
+        self.spread()
+
+    def spread(self):
         h = self.here
-        self.go(0, h.me, h.opp)
         self.go(1, h.me, h.right)
         self.go(2, h.me, h.left)
+        self.go(5, h.me, h.far)
         self.go(7, h.me, h.sib)
 
     def across(self):
+        for part in range(self.parts):
+            self.got(0, self.here.opp, part)
+            self.spread_opp(part)
+        self.go(8, self.here.opp, self.here.sib)
+
+    def spread_opp(self, part):
         h = self.here
-        self.got(0, h.opp)
-        self.go(3, h.opp, h.right)
-        self.go(4, h.opp, h.left)
-        self.go(8, h.opp, h.sib)
+        self.go(3, h.opp, h.right, part)
+        self.go(4, h.opp, h.left, part)
+        self.go(6, h.opp, h.far, part)
 
     def near(self):
         h = self.here
-        self.got(1, h.left)
-        self.go(5, h.left, h.right)
-        self.go(9, h.left, h.sib)
-        self.got(2, h.right)
-        self.go(10, h.right, h.sib)
+        for kind, slot, onward in ((1, h.left, 9), (2, h.right, 10), (5, h.far, 13)):
+            self.got(kind, slot)
+            self.go(onward, slot, h.sib)
 
     def near_opp(self):
         h = self.here
-        self.got(4, h.right_opp)
-        self.go(6, h.right_opp, h.left)
-        self.go(11, h.right_opp, h.sib)
-        self.got(3, h.left_opp)
-        self.go(12, h.left_opp, h.sib)
-
-    def far(self):
-        h = self.here
-        self.got(5, h.far)
-        self.go(13, h.far, h.sib)
-
-    def far_opp(self):
-        h = self.here
-        self.got(6, h.far_opp)
-        self.go(14, h.far_opp, h.sib)
+        for kind, slot, onward in ((3, h.left_opp, 11), (4, h.right_opp, 12), (6, h.far_opp, 14)):
+            for part in range(self.parts):
+                self.got(kind, slot, part)
+            self.go(onward, slot, h.sib)
 
     def plane(self):
         h = self.here
@@ -121,8 +123,8 @@
     def plane_opp(self):
         h = self.here
         self.got(8, h.other(h.opp))
-        self.got(11, h.other(h.right_opp))
-        self.got(12, h.other(h.left_opp))
+        self.got(11, h.other(h.left_opp))
+        self.got(12, h.other(h.right_opp))
         self.got(14, h.other(h.far_opp))
 
     def drain(self):
@@ -158,8 +160,8 @@
 
 def main_kernel(
     label, partner_h, x_h, w3s_h, w1s_h, hds_h, w3t_h, w1t_h, hdt_h,
-    xeo, hc, dz_out, dpre_out, dl_out, pooled_out,
-    partner, x, w3s, w3t, wxs, wxt, w1raw, w1p, hds, hdt, xg, xgt, hg, hgt, accs, acct,
+    xeo, dpre_out, gw1_out, gh_out,
+    partner, x, hc, w3s, w3t, wxs, wxt, w1raw, w1p, hds, hdt, xg, xgt, hg, hgt, accs, acct,
     a1, sb, ls, lt, ua, row, sendb, block, ra, rb, rc,
     wsem, gsend, grecv, asend, arecv, lsend, lrecv, rsend, rrecv,
 ):
@@ -199,24 +201,23 @@
     inside = lane_to % 64
     perm = jnp.where((inside < HALF) & (lane_from == 2 * inside + lane_to // 64), 1.0, 0.0)
     perm = perm.astype(BF16)
-    own = pl.ds(pl.multiple_of(me * LANES, LANES), LANES)
     loads[0].wait()
-    xg[:, own] = mm(x[...], perm).astype(BF16)
+    xg[me] = mm(x[...], perm).astype(BF16)
 
     pl.semaphore_wait(barrier, N_REP - 1 + N_FILT - 1)
 
     gx = Gather(xg, gsend.at[0], grecv.at[0], h)
     gxt = Gather(xgt, gsend.at[1], grecv.at[1], h)
     gh = Gather(hg, gsend.at[2], grecv.at[2], h)
-    ght = Gather(hgt, gsend.at[3], grecv.at[3], h)
+    ght = Gather(hgt, gsend.at[3], grecv.at[3], h, 2)
 
     for i in range(1, N_REP):
         q = (rep + i) % N_REP
 
-        @pl.when(q < CHUNKS)
+        @pl.when((q % 2 == 0) & (q < 2 * CHUNKS))
         def _():
             pltpu.make_async_remote_copy(
-                src_ref=xg.at[pl.ds(pl.multiple_of(q * RELAY, RELAY), RELAY), own],
+                src_ref=xg.at[me, pl.ds(pl.multiple_of(q // 2 * RELAY, RELAY), RELAY)],
                 dst_ref=a1.at[rep],
                 send_sem=asend.at[0],
                 recv_sem=arecv.at[0],
@@ -246,54 +247,58 @@
 
         lax.fori_loop(first, last, body, 0)
 
-    chunk = pl.ds(pl.multiple_of(rep * RELAY, RELAY), RELAY)
+    relay = (rep % 2 == 0) & (rep < 2 * CHUNKS)
+    chunk = pl.ds(pl.multiple_of(rep % (2 * CHUNKS) // 2 * RELAY, RELAY), RELAY)
     loads[2].wait()
     ordered(w3s, wxs, 0, 3)
 
-    @pl.when(rep < CHUNKS)
+    @pl.when(relay)
     def _():
         pltpu.make_async_copy(a1.at[pl.ds(0, 15)], a1.at[pl.ds(0, 15)], arecv.at[0]).wait()
-        a1[rep] = xg[chunk, own]
-        xgt[chunk, own] = a1[partner[rep]]
-        for i in range(1, N_REP):
+        a1[rep] = xg[me, chunk]
+        xgt[me, chunk] = a1[partner[rep]]
+        for i in range(N_REP):
             p = (rep + i) % N_REP
             sb[i] = a1[partner[p]]
-            pltpu.make_async_remote_copy(
-                src_ref=sb.at[i],
-                dst_ref=xgt.at[chunk, own],
-                send_sem=asend.at[1],
-                recv_sem=arecv.at[1],
-                device_id={"rep": p, "filt": me},
-                device_id_type=MESH,
-            ).start()
+            for plane, target in enumerate((h.opp, me)):
+                if i > 0 or plane == 0:
+                    pltpu.make_async_remote_copy(
+                        src_ref=sb.at[i],
+                        dst_ref=xgt.at[me, chunk],
+                        send_sem=asend.at[1 + 2 * plane],
+                        recv_sem=arecv.at[1 + 2 * plane],
+                        device_id={"rep": p, "filt": target},
+                        device_id_type=MESH,
+                    ).start()
 
     gx.near()
-    ordered(w3s, wxs, 3, 6)
-    gx.far()
+    ordered(w3s, wxs, 3, 7)
     gx.across()
 
-    @pl.when(rep < CHUNKS)
+    @pl.when(relay)
     def _():
         pltpu.make_async_copy(
-            xgt.at[pl.ds(0, RELAY * (CHUNKS - 1)), own],
-            xgt.at[pl.ds(0, RELAY * (CHUNKS - 1)), own],
-            arecv.at[1],
+            xgt.at[me, pl.ds(0, RELAY * (CHUNKS - 1))],
+            xgt.at[me, pl.ds(0, RELAY * (CHUNKS - 1))],
+            arecv.at[3],
         ).wait()
 
-    @pl.when(rep >= CHUNKS)
+    @pl.when(jnp.logical_not(relay))
     def _():
-        pltpu.make_async_copy(xgt.at[:, own], xgt.at[:, own], arecv.at[1]).wait()
-
-    gxt.own()
-    ordered(w3s, wxs, 6, 9)
-    gx.near_opp()
-    gx.far_opp()
+        pltpu.make_async_copy(xgt.at[me], xgt.at[me], arecv.at[3]).wait()
+
+    gxt.spread()
+    pltpu.make_async_copy(xgt.at[h.opp], xgt.at[h.opp], arecv.at[1]).wait()
+    gxt.spread_opp(0)
+    gxt.go(8, h.opp, h.sib)
+    ordered(w3s, wxs, 7, 9)
 
     def conv_half(panel, wx, acc, z, first):
         rows = pl.ds(pl.multiple_of(z * (8 * LANES), 8 * LANES), 8 * LANES)
+        left = jnp.concatenate([panel[z * 8 + i] for i in range(8)], axis=1)
         for i in range(3):
             where = slice(i * 3 * LANES, (i + 1) * 3 * LANES)
-            part = mm(panel[:, rows], wx[rows, where])
+            part = mm(left, wx[rows, where])
             acc[:, where] = part if first else acc[:, where] + part
 
     lanes = lax.broadcasted_iota(jnp.int32, (POS, LANES), 1)
@@ -320,29 +325,27 @@
     def hidden_of(pre):
         return jnp.where(lanes < LOC, silu(pre), 0.0).astype(BF16)
 
-    gxt.near()
     gx.plane()
     conv_half(xg, wxs, accs, h.z, True)
-    gxt.far()
-    gxt.across()
+    loads[3].wait()
+    ordered(w3t, wxt, 0, 3)
+    gxt.near()
+    gx.near_opp()
+    ordered(w3t, wxt, 3, 6)
     gx.plane_opp()
     conv_half(xg, wxs, accs, 1 - h.z, False)
+    gxt.near_opp()
     pre = conv_end(accs)
-    hg[:, own] = hidden_of(pre)
+    hg[me] = hidden_of(pre)
     gh.own()
-    gxt.near_opp()
-    loads[3].wait()
-    ordered(w3t, wxt, 0, 4)
-    gxt.far_opp()
-    ordered(w3t, wxt, 4, 9)
-    gh.near()
+    ordered(w3t, wxt, 6, 9)
     gxt.plane()
     conv_half(xgt, wxt, acct, h.z, True)
-    gh.far()
     gxt.plane_opp()
     conv_half(xgt, wxt, acct, 1 - h.z, False)
-    hgt[:, own] = hidden_of(conv_end(acct))
+    hgt[me] = hidden_of(conv_end(acct))
     ght.own()
+    gh.near()
     gh.across()
 
     for which in range(2):
@@ -353,11 +356,13 @@
 
     gh.near_opp()
     ght.near()
-    gh.far_opp()
-    ght.far()
     ght.across()
     gh.plane()
     gh.plane_opp()
+    ght.near_opp()
+
+    def whole(panel):
+        return jnp.concatenate([panel[i] for i in range(N_FILT)], axis=1)
 
     def logits_of(z, head):
         pooled = jnp.sum(silu(z), axis=0, keepdims=True) * (1.0 / POS)
@@ -390,18 +395,16 @@
 
     loads[6].wait()
     loads[7].wait()
-    z_mixed = x[...].astype(F32) + mm(hg[...], w1p[0])
+    z_mixed = x[...].astype(F32) + mm(whole(hg), w1p[0])
     pooled, part = logits_of(z_mixed, hds)
     give_logits(ls, part, 0)
-    ght.near_opp()
-    ght.far_opp()
-    xt = mm(xgt[:, own], perm, ((1,), (1,)))
+    xt = mm(xgt[me], perm, ((1,), (1,)))
     ght.plane()
     ght.plane_opp()
-    part = logits_of(xt + mm(hgt[...], w1p[1]), hdt)[1]
+    part = logits_of(xt + mm(whole(hgt), w1p[1]), hdt)[1]
     give_logits(lt, part, 1)
     for f in range(N_FILT):
-        hc[:, f * LOC : (f + 1) * LOC] = hg[:, f * LANES : f * LANES + LOC]
+        hc[:, f * LOC : (f + 1) * LOC] = hg[f, :, :LOC]
     logits = sum_logits(ls, 0)
 
     cls = lax.broadcasted_iota(jnp.int32, (8, LANES), 0) * LANES + lax.broadcasted_iota(
@@ -426,19 +429,16 @@
             device_id={"rep": (rep + i) % N_REP, "filt": me},
             device_id_type=MESH,
         ).start()
-    pooled_out[...] = pooled
     for f in range(N_FILT):
         for g in range(2):
             xeo[g * POS : (g + 1) * POS, f * HALF : (f + 1) * HALF] = xg[
-                :, f * LANES + 64 * g : f * LANES + 64 * g + HALF
+                f, :, 64 * g : 64 * g + HALF
             ]
     wait_bytes(ua, N_REP - 1, arecv.at[2])
     dl = own_part - softmax(ua[partner[rep]])
-    dl_out[...] = dl
     dl_row = jnp.concatenate([dl[i : i + 1, :] for i in range(8)], axis=1)[:, :K]
     parts = mm(split3(dl_row), hds[...])
     dz = ((parts[0:1] + parts[1:2] + parts[2:3]) * slope).astype(BF16)
-    dz_out[...] = dz
 
     def remote(src, dst, kind, target):
         return pltpu.make_async_remote_copy(
@@ -450,65 +450,62 @@
             device_id_type=MESH,
         )
 
-    targets = (
-        h.at(0, h.beyond, h.k),
-        h.at(1, h.beyond, h.k),
-        h.at(0, h.up, h.k),
-        h.at(1, h.down, h.k),
-        h.at(1, h.up, h.k),
-        h.at(0, h.down, h.k),
-        h.opp,
-        me,
-    )
+    zz = 1 - h.z
+    ya = (h.y + 1 + 2 * zz) % 4
+    yb = (h.y + 1 + 2 * h.z) % 4
+    side_a = h.at(h.z, ya, h.k)
+    side_b = h.at(h.z, yb, h.k)
     mine_at = pl.ds(pl.multiple_of(h.k * LANES, LANES), LANES)
     other_at = pl.ds(pl.multiple_of((1 - h.k) * LANES, LANES), LANES)
-    for z in range(2):
-        rows = slice(z * 8 * LANES, (z + 1) * 8 * LANES)
+    places = ((h.beyond, yb, ya, h.y), (h.beyond, ya, yb, h.y))
+    sib_copies = []
+    for i, z in enumerate((zz, h.z)):
+        rows = pl.ds(pl.multiple_of(z * 8 * LANES, 8 * LANES), 8 * LANES)
         part = mm(dz, w1p[0, rows, :], ((1,), (1,)))
         for y in range(4):
-            block[z * 4 + y] = part[:, y * 2 * LANES : (y + 1) * 2 * LANES]
-    sib_copies = []
-    for i, slot in enumerate(targets):
-        sendb[i] = block[slot // 2, :, other_at].astype(BF16)
-        made = remote(sendb.at[i], ra.at[i], i, h.sib)
-        made.start()
-        sib_copies.append(made)
-
-    def chip_sum(i):
-        sib_copies[i].wait_recv()
-        return block[targets[i] // 2, :, mine_at] + ra[i].astype(F32)
+            block[i * 4 + y] = part[:, y * 2 * LANES : (y + 1) * 2 * LANES]
+        for j, y in enumerate(places[i]):
+            sendb[i * 4 + j] = block[i * 4 + y, :, other_at].astype(BF16)
+            made = remote(sendb.at[i * 4 + j], ra.at[i * 4 + j], i * 4 + j, h.sib)
+            made.start()
+            sib_copies.append(made)
+
+    def chip_sum(i, j):
+        sib_copies[i * 4 + j].wait_recv()
+        return block[i * 4 + places[i][j], :, mine_at] + ra[i * 4 + j].astype(F32)
 
     ring = []
 
-    def ring_send(i, value, target):
+    def ring_send(value, target):
+        i = len(ring)
         sendb[8 + i] = value.astype(BF16)
         made = remote(sendb.at[8 + i], rb.at[i], 8 + i, target)
         made.start()
         ring.append(made)
 
-    ring_send(0, chip_sum(0), h.right)
-    ring_send(1, chip_sum(1), h.left)
-    ring_send(2, chip_sum(4), h.right)
-    ring_send(3, chip_sum(5), h.left)
-    up0 = chip_sum(2)
-    down1 = chip_sum(3)
-    ring[0].wait_recv()
-    ring_send(4, up0 + rb[0].astype(F32), h.right)
-    ring[1].wait_recv()
-    ring_send(5, down1 + rb[1].astype(F32), h.left)
-    to_opp = chip_sum(6)
-    mine = chip_sum(7)
-    ring[2].wait_recv()
-    ring[3].wait_recv()
-    ring[4].wait_recv()
-    ring[5].wait_recv()
-    low = h.z == 0
-    sum0 = rb[4].astype(F32) + rb[3].astype(F32)
-    sum1 = rb[5].astype(F32) + rb[2].astype(F32)
-    sendb[14] = (to_opp + jnp.where(low, sum1, sum0)).astype(BF16)
+    def arrived(i):
+        ring[i].wait_recv()
+        return rb[i].astype(F32)
+
+    ring_send(chip_sum(0, 0), side_a)
+    ring_send(chip_sum(0, 1), side_b)
+    ring_send(chip_sum(1, 0), side_b)
+    ring_send(chip_sum(1, 1), side_a)
+    onward = chip_sum(0, 2)
+    ring_send(onward + arrived(0), side_a)
+    onward = chip_sum(1, 2)
+    ring_send(onward + arrived(2), side_b)
+    to_opp = chip_sum(0, 3) + arrived(1)
+    sendb[14] = (to_opp + arrived(4)).astype(BF16)
     last = remote(sendb.at[14], rc, 14, h.opp)
     last.start()
-    mine = mine + jnp.where(low, sum0, sum1)
+    mine = chip_sum(1, 3) + arrived(3)
+    mine = mine + arrived(5)
+    gw1_out[...] = mm(dz, hc[...], ((0,), (0,)))
+    flip = dl.T
+    for i in range(8):
+        size = min(LANES, K - i * LANES)
+        gh_out[i * LANES : i * LANES + size, :] = flip[:size, i : i + 1] * pooled
     slope = dsilu(pre)
     last.wait_recv()
     dhidden = mine + rc[...].astype(F32)
@@ -522,17 +519,18 @@
     wait_bytes(lt, N_FILT - 1, lsend.at[1])
     wait_bytes(ua, N_REP - 1, asend.at[2])
 
-    @pl.when(rep < CHUNKS)
+    @pl.when(relay)
     def _():
         wait_bytes(sb, CHUNKS - 1, asend.at[0])
-        wait_bytes(sb, N_REP - 1, asend.at[1])
-
-    @pl.when(rep >= CHUNKS)
+        wait_bytes(sb, N_REP, asend.at[1])
+        wait_bytes(sb, N_REP - 1, asend.at[3])
+
+    @pl.when(jnp.logical_not(relay))
     def _():
         wait_bytes(sb, CHUNKS, asend.at[0])
 
 
-def grads_kernel(xeo, hc, dz, dpre, dl, pooled, gw3, gw1, gh, turned, r3, r1, r0, sem):
+def grads_kernel(xeo, dpre, r1, r0, gw3, gw1, gh, turned, r3, sem):
     copies = []
 
     def out(src, dst, i):
@@ -540,6 +538,8 @@
         made.start()
         copies.append(made)
 
+    out(r1, gw1.at[:, 0, :], 9)
+    out(r0, gh, 10)
     dp = dpre[...].astype(F32)
     even = lax.broadcasted_iota(jnp.int32, (POS, LOC), 1) % 2 == 0
     column = lax.broadcasted_iota(jnp.int32, (POS, LOC), 0) % MAP_W
@@ -565,13 +565,6 @@
             t = 3 * a + b
             r3[t] = rows[a * LANES : a * LANES + LOC]
             out(r3.at[t], gw3.at[:, t, 0, :], t)
-    r1[...] = mm(dz[...], hc[...], ((0,), (0,)))
-    out(r1, gw1.at[:, 0, :], 9)
-    flip = dl[...].T
-    for i in range(8):
-        size = min(LANES, K - i * LANES)
-        r0[i * LANES : i * LANES + size, :] = flip[:size, i : i + 1] * pooled[...]
-    out(r0, gh, 10)
     for made in copies:
         made.wait()
 
@@ -593,17 +586,16 @@
         main_kernel,
         out_shape=(
             pltpu.VMEM((2 * POS, GW), BF16),
-            pltpu.VMEM((POS, C), BF16),
             pltpu.VMEM((POS, LOC), BF16),
-            pltpu.VMEM((POS, LOC), BF16),
-            pltpu.VMEM((8, LANES), F32),
-            pltpu.VMEM((1, LOC), F32),
+            pltpu.VMEM((LOC, C), F32),
+            pltpu.VMEM((K, LOC), F32),
         ),
         in_specs=[pl.BlockSpec(memory_space=pltpu.SMEM)] + [hbm] * 8,
-        out_specs=[vmem] * 6,
+        out_specs=[vmem] * 4,
         scratch_shapes=[
             pltpu.SMEM((N_REP,), jnp.int32),
             pltpu.VMEM((POS, LOC), BF16),
+            pltpu.VMEM((POS, C), BF16),
             pltpu.VMEM((9, GW, LOC), BF16),
             pltpu.VMEM((9, GW, LOC), BF16),
             pltpu.VMEM((N_FILT * LANES, 9 * LANES), BF16),
@@ -612,10 +604,10 @@
             pltpu.VMEM((2, N_FILT * LANES, LOC), BF16),
             pltpu.VMEM((K, LOC), BF16),
             pltpu.VMEM((K, LOC), BF16),
-            pltpu.VMEM((POS, N_FILT * LANES), BF16),
-            pltpu.VMEM((POS, N_FILT * LANES), BF16),
-            pltpu.VMEM((POS, N_FILT * LANES), BF16),
-            pltpu.VMEM((POS, N_FILT * LANES), BF16),
+            pltpu.VMEM((N_FILT, POS, LANES), BF16),
+            pltpu.VMEM((N_FILT, POS, LANES), BF16),
+            pltpu.VMEM((N_FILT, POS, LANES), BF16),
+            pltpu.VMEM((N_FILT, POS, LANES), BF16),
             pltpu.VMEM((POS, 9 * LANES), F32),
             pltpu.VMEM((POS, 9 * LANES), F32),
             pltpu.VMEM((N_REP, RELAY, LANES), BF16),
@@ -630,10 +622,10 @@
             pltpu.VMEM((6, POS, LANES), BF16),
             pltpu.VMEM((POS, LANES), BF16),
             dma((8,)),
-            dma((4, 15)),
-            dma((4, 15)),
-            dma((3,)),
-            dma((3,)),
+            dma((4, 19)),
+            dma((4, 19)),
+            dma((4,)),
+            dma((4,)),
             dma((2,)),
             dma((2,)),
             dma((15,)),
@@ -657,13 +649,11 @@
             sds((LOC, 1, C), F32),
             sds((K, LOC), F32),
         ),
-        in_specs=[vmem] * 6,
+        in_specs=[vmem] * 4,
         out_specs=[hbm] * 3,
         scratch_shapes=[
             pltpu.VMEM((3, 2 * POS, 3 * LANES), BF16),
             pltpu.VMEM((9, LOC, GW), F32),
-            pltpu.VMEM((LOC, C), F32),
-            pltpu.VMEM((K, LOC), F32),
             dma((11,)),
         ],
         compiler_params=pltpu.CompilerParams(vmem_limit_bytes=40 * 1024 * 1024),

time: 92.7 us -> 80.5 us (0.87)
  Pallas kernels: 91.4 us -> 78.3 us
    pallas_call x1, Pallas kernels: 87.7 us -> 75.1 us  [per_device(): pl.pallas_call(main_kernel, out_shape=(pltpu.VMEM((2 * POS, GW), BF16), p...]
where the time goes in v2:
time: 80.5 us; the launch traced here: 79.5 us
  Pallas kernels  78.3 us (97%)
  between operations  1.29 us (2%)
    pallas_call x1, Pallas kernels, per_device(): pl.pallas_call(main_kernel, out_shape=(pltpu.VMEM((2 * POS, GW), BF16), p...  75.1 us
    pallas_call x1, Pallas kernels, per_device(): pl.pallas_call(grads_kernel, out_shape=(sds((LOC, 9, 1, GW), F32), sds((L...  3.12 us

profile of v2, /device:TPU:1, one launch (start us, length us, event | category | flops | bytes accessed | tf_op | source)
XLA Modules:
  0.0 79.5 jit_solution(2923562001470129010)
XLA Ops:
  1.3 75.1 %step.1 = (bf16[448,1008]{1,0:T(8,128)(2,1)S(1)}, bf16[224,126]{1,0:T(8,128)(2,1)S(1)}, f32[126,2016]{1,0:T(8,128)S(1)}, f32[1000,126]{1,0:T(8,128)S(1)}) custom-call(s32[1]{0:T(128)S(6)} %copy.12.label, s32[16]{0:T(128)} %partner_h.1, bf16[224,126]{1,0:T(8,128)(2,1)} %bitcast.32, bf16[9,1008,126]{2,1,0:T(8,128)(2,1)} %bitcast.26, ...), custom_call_target="tpu_custom_call" | custom-call | tf_op jit(solution)/shard_map/step/pallas_call | solution.py:585
  76.4 3.1 %grads.1 = (f32[126,9,1,1008]{3,2,1,0:T(1,128)}, f32[126,1,2016]{2,1,0:T(1,128)}, f32[1000,126]{1,0:T(8,128)}) custom-call(bf16[448,1008]{1,0:T(8,128)(2,1)S(1)} %get-tuple-element.10.xeo, bf16[224,126]{1,0:T(8,128)(2,1)S(1)} %get-tuple-element.11.dpre, f32[126,2016]{1,0:T(8,128)S(1)} %get-tuple-element.12.r1, f32[1000,126]{1,0:T(8,128)S(1)} %get-tuple-element.13.r0), custom_call_target="tpu_custom_call" | custom-call | tf_op jit(solution)/shard_map/grads/pallas_call | solution.py:645

commit v3 on v2

--- a/solution.py
+++ b/solution.py
@@ -161,7 +161,7 @@
 def main_kernel(
     label, partner_h, x_h, w3s_h, w1s_h, hds_h, w3t_h, w1t_h, hdt_h,
     xeo, dpre_out, gw1_out, gh_out,
-    partner, x, hc, w3s, w3t, wxs, wxt, w1raw, w1p, hds, hdt, xg, xgt, hg, hgt, accs, acct,
+    partner, x, xraw, hc, w3s, w3t, wxs, wxt, w1raw, w1p, hds, hdt, xg, xgt, hg, hgt, accs, acct,
     a1, sb, ls, lt, ua, row, sendb, block, ra, rb, rc,
     wsem, gsend, grecv, asend, arecv, lsend, lrecv, rsend, rrecv,
 ):
@@ -201,9 +201,6 @@
     inside = lane_to % 64
     perm = jnp.where((inside < HALF) & (lane_from == 2 * inside + lane_to // 64), 1.0, 0.0)
     perm = perm.astype(BF16)
-    loads[0].wait()
-    xg[me] = mm(x[...], perm).astype(BF16)
-
     pl.semaphore_wait(barrier, N_REP - 1 + N_FILT - 1)
 
     gx = Gather(xg, gsend.at[0], grecv.at[0], h)
@@ -217,7 +214,7 @@
         @pl.when((q % 2 == 0) & (q < 2 * CHUNKS))
         def _():
             pltpu.make_async_remote_copy(
-                src_ref=xg.at[me, pl.ds(pl.multiple_of(q // 2 * RELAY, RELAY), RELAY)],
+                src_ref=x_h.at[pl.ds(pl.multiple_of(q // 2 * RELAY, RELAY), RELAY)],
                 dst_ref=a1.at[rep],
                 send_sem=asend.at[0],
                 recv_sem=arecv.at[0],
@@ -225,6 +222,8 @@
                 device_id_type=MESH,
             ).start()
 
+    loads[0].wait()
+    xg[me] = mm(x[...], perm).astype(BF16)
     gx.own()
     loads[1].wait()
 
@@ -250,13 +249,13 @@
     relay = (rep % 2 == 0) & (rep < 2 * CHUNKS)
     chunk = pl.ds(pl.multiple_of(rep % (2 * CHUNKS) // 2 * RELAY, RELAY), RELAY)
     loads[2].wait()
-    ordered(w3s, wxs, 0, 3)
+    ordered(w3s, wxs, 0, 4)
 
     @pl.when(relay)
     def _():
         pltpu.make_async_copy(a1.at[pl.ds(0, 15)], a1.at[pl.ds(0, 15)], arecv.at[0]).wait()
-        a1[rep] = xg[me, chunk]
-        xgt[me, chunk] = a1[partner[rep]]
+        a1[rep] = x[chunk]
+        xraw[0, chunk] = a1[partner[rep]]
         for i in range(N_REP):
             p = (rep + i) % N_REP
             sb[i] = a1[partner[p]]
@@ -264,7 +263,7 @@
                 if i > 0 or plane == 0:
                     pltpu.make_async_remote_copy(
                         src_ref=sb.at[i],
-                        dst_ref=xgt.at[me, chunk],
+                        dst_ref=xraw.at[1 - plane, chunk],
                         send_sem=asend.at[1 + 2 * plane],
                         recv_sem=arecv.at[1 + 2 * plane],
                         device_id={"rep": p, "filt": target},
@@ -272,26 +271,31 @@
                     ).start()
 
     gx.near()
-    ordered(w3s, wxs, 3, 7)
+    ordered(w3s, wxs, 4, 8)
     gx.across()
+    ordered(w3s, wxs, 8, 9)
+    loads[3].wait()
+    ordered(w3t, wxt, 0, 2)
 
     @pl.when(relay)
     def _():
         pltpu.make_async_copy(
-            xgt.at[me, pl.ds(0, RELAY * (CHUNKS - 1))],
-            xgt.at[me, pl.ds(0, RELAY * (CHUNKS - 1))],
+            xraw.at[0, pl.ds(0, RELAY * (CHUNKS - 1))],
+            xraw.at[0, pl.ds(0, RELAY * (CHUNKS - 1))],
             arecv.at[3],
         ).wait()
 
     @pl.when(jnp.logical_not(relay))
     def _():
-        pltpu.make_async_copy(xgt.at[me], xgt.at[me], arecv.at[3]).wait()
-
+        pltpu.make_async_copy(xraw.at[0], xraw.at[0], arecv.at[3]).wait()
+
+    xgt[me] = mm(xraw[0], perm).astype(BF16)
     gxt.spread()
-    pltpu.make_async_copy(xgt.at[h.opp], xgt.at[h.opp], arecv.at[1]).wait()
+    pltpu.make_async_copy(xraw.at[1], xraw.at[1], arecv.at[1]).wait()
+    xgt[h.opp] = mm(xraw[1], perm).astype(BF16)
     gxt.spread_opp(0)
     gxt.go(8, h.opp, h.sib)
-    ordered(w3s, wxs, 7, 9)
+    ordered(w3t, wxt, 2, 5)
 
     def conv_half(panel, wx, acc, z, first):
         rows = pl.ds(pl.multiple_of(z * (8 * LANES), 8 * LANES), 8 * LANES)
@@ -327,18 +331,15 @@
 
     gx.plane()
     conv_half(xg, wxs, accs, h.z, True)
-    loads[3].wait()
-    ordered(w3t, wxt, 0, 3)
     gxt.near()
     gx.near_opp()
-    ordered(w3t, wxt, 3, 6)
+    ordered(w3t, wxt, 5, 9)
     gx.plane_opp()
     conv_half(xg, wxs, accs, 1 - h.z, False)
     gxt.near_opp()
     pre = conv_end(accs)
     hg[me] = hidden_of(pre)
     gh.own()
-    ordered(w3t, wxt, 6, 9)
     gxt.plane()
     conv_half(xgt, wxt, acct, h.z, True)
     gxt.plane_opp()
@@ -376,7 +377,7 @@
 
     def give_logits(buf, part, idx):
         buf[me] = part
-        for i in range(1, N_FILT):
+        for i in (8, 7, 9, 6, 10, 5, 11, 4, 12, 3, 13, 2, 14, 1, 15):
             pltpu.make_async_remote_copy(
                 src_ref=buf.at[me],
                 dst_ref=buf.at[me],
@@ -398,7 +399,7 @@
     z_mixed = x[...].astype(F32) + mm(whole(hg), w1p[0])
     pooled, part = logits_of(z_mixed, hds)
     give_logits(ls, part, 0)
-    xt = mm(xgt[me], perm, ((1,), (1,)))
+    xt = xraw[0].astype(F32)
     ght.plane()
     ght.plane_opp()
     part = logits_of(xt + mm(whole(hgt), w1p[1]), hdt)[1]
@@ -451,69 +452,73 @@
         )
 
     zz = 1 - h.z
-    ya = (h.y + 1 + 2 * zz) % 4
-    yb = (h.y + 1 + 2 * h.z) % 4
-    side_a = h.at(h.z, ya, h.k)
-    side_b = h.at(h.z, yb, h.k)
     mine_at = pl.ds(pl.multiple_of(h.k * LANES, LANES), LANES)
     other_at = pl.ds(pl.multiple_of((1 - h.k) * LANES, LANES), LANES)
-    places = ((h.beyond, yb, ya, h.y), (h.beyond, ya, yb, h.y))
+    places = (h.beyond, h.up, h.down, h.y)
     sib_copies = []
     for i, z in enumerate((zz, h.z)):
         rows = pl.ds(pl.multiple_of(z * 8 * LANES, 8 * LANES), 8 * LANES)
         part = mm(dz, w1p[0, rows, :], ((1,), (1,)))
         for y in range(4):
             block[i * 4 + y] = part[:, y * 2 * LANES : (y + 1) * 2 * LANES]
-        for j, y in enumerate(places[i]):
+        for j, y in enumerate(places):
             sendb[i * 4 + j] = block[i * 4 + y, :, other_at].astype(BF16)
             made = remote(sendb.at[i * 4 + j], ra.at[i * 4 + j], i * 4 + j, h.sib)
             made.start()
             sib_copies.append(made)
 
-    def chip_sum(i, j):
-        sib_copies[i * 4 + j].wait_recv()
-        return block[i * 4 + places[i][j], :, mine_at] + ra[i * 4 + j].astype(F32)
-
-    ring = []
-
-    def ring_send(value, target):
-        i = len(ring)
-        sendb[8 + i] = value.astype(BF16)
-        made = remote(sendb.at[8 + i], rb.at[i], 8 + i, target)
+    mid = POS // 2
+    halves = (slice(0, mid), slice(mid, POS))
+
+    def chip_sum(i, j, rows):
+        return block[i * 4 + places[j], rows, mine_at] + ra[i * 4 + j, rows].astype(F32)
+
+    side = [h.at(h.z, y, h.k) for y in places[:3]]
+    across = []
+    for half, rows in enumerate(halves):
+        for j in range(3):
+            if half == 0:
+                sib_copies[j].wait_recv()
+            sendb[8 + j, rows] = chip_sum(0, j, rows).astype(BF16)
+            made = remote(sendb.at[8 + j, rows], rb.at[j, rows], 8 + half * 3 + j, side[j])
+            made.start()
+            across.append(made)
+    for j in range(3):
+        sib_copies[4 + j].wait_recv()
+        sendb[11 + j] = chip_sum(1, j, slice(0, POS)).astype(BF16)
+        made = remote(sendb.at[11 + j], rb.at[3 + j], 14 + j, side[j])
         made.start()
-        ring.append(made)
-
-    def arrived(i):
-        ring[i].wait_recv()
-        return rb[i].astype(F32)
-
-    ring_send(chip_sum(0, 0), side_a)
-    ring_send(chip_sum(0, 1), side_b)
-    ring_send(chip_sum(1, 0), side_b)
-    ring_send(chip_sum(1, 1), side_a)
-    onward = chip_sum(0, 2)
-    ring_send(onward + arrived(0), side_a)
-    onward = chip_sum(1, 2)
-    ring_send(onward + arrived(2), side_b)
-    to_opp = chip_sum(0, 3) + arrived(1)
-    sendb[14] = (to_opp + arrived(4)).astype(BF16)
-    last = remote(sendb.at[14], rc, 14, h.opp)
-    last.start()
-    mine = chip_sum(1, 3) + arrived(3)
-    mine = mine + arrived(5)
+        across.append(made)
+    sib_copies[3].wait_recv()
+    last = []
+    for half, rows in enumerate(halves):
+        total = chip_sum(0, 3, rows)
+        for j in (1, 2, 0):
+            across[half * 3 + j].wait_recv()
+            total = total + rb[j, rows].astype(F32)
+        sendb[14, rows] = total.astype(BF16)
+        made = remote(sendb.at[14, rows], rc.at[rows], 17 + half, h.opp)
+        made.start()
+        last.append(made)
+    sib_copies[7].wait_recv()
+    mine = chip_sum(1, 3, slice(0, POS))
+    for j in (1, 2, 0):
+        across[6 + j].wait_recv()
+        mine = mine + rb[3 + j].astype(F32)
     gw1_out[...] = mm(dz, hc[...], ((0,), (0,)))
     flip = dl.T
     for i in range(8):
         size = min(LANES, K - i * LANES)
         gh_out[i * LANES : i * LANES + size, :] = flip[:size, i : i + 1] * pooled
     slope = dsilu(pre)
-    last.wait_recv()
+    for made in last:
+        made.wait_recv()
     dhidden = mine + rc[...].astype(F32)
     dpre_out[...] = (dhidden * slope)[:, :LOC].astype(BF16)
 
     for gather in (gx, gxt, gh, ght):
         gather.drain()
-    for made in sib_copies + ring + [last]:
+    for made in sib_copies + across + last:
         made.wait_send()
     wait_bytes(ls, N_FILT - 1, lsend.at[0])
     wait_bytes(lt, N_FILT - 1, lsend.at[1])
@@ -595,6 +600,7 @@
         scratch_shapes=[
             pltpu.SMEM((N_REP,), jnp.int32),
             pltpu.VMEM((POS, LOC), BF16),
+            pltpu.VMEM((2, POS, LOC), BF16),
             pltpu.VMEM((POS, C), BF16),
             pltpu.VMEM((9, GW, LOC), BF16),
             pltpu.VMEM((9, GW, LOC), BF16),
@@ -610,8 +616,8 @@
             pltpu.VMEM((N_FILT, POS, LANES), BF16),
             pltpu.VMEM((POS, 9 * LANES), F32),
             pltpu.VMEM((POS, 9 * LANES), F32),
-            pltpu.VMEM((N_REP, RELAY, LANES), BF16),
-            pltpu.VMEM((N_REP, RELAY, LANES), BF16),
+            pltpu.VMEM((N_REP, RELAY, LOC), BF16),
+            pltpu.VMEM((N_REP, RELAY, LOC), BF16),
             pltpu.VMEM((N_FILT, 8, LANES), F32),
             pltpu.VMEM((N_FILT, 8, LANES), F32),
             pltpu.VMEM((N_REP, 8, LANES), F32),
@@ -628,8 +634,8 @@
             dma((4,)),
             dma((2,)),
             dma((2,)),
-            dma((15,)),
-            dma((15,)),
+            dma((19,)),
+            dma((19,)),
         ],
         compiler_params=pltpu.CompilerParams(
             collective_id=0, has_side_effects=True, vmem_limit_bytes=48 * 1024 * 1024

time: 80.5 us -> 79.6 us (0.989); the launches traced: 79.5 us -> 79.5 us
  no operation moved by 1% of the time
where the time goes in v3:
time: 79.6 us; the launch traced here: 79.5 us
  Pallas kernels  78.2 us (98%)
  between operations  1.29 us (2%)
    pallas_call x1, Pallas kernels, per_device(): pl.pallas_call(main_kernel, out_shape=(pltpu.VMEM((2 * POS, GW), BF16), p...  75.1 us
    pallas_call x1, Pallas kernels, per_device(): pl.pallas_call(grads_kernel, out_shape=(sds((LOC, 9, 1, GW), F32), sds((L...  3.11 us

profile of v3, /device:TPU:1, one launch (start us, length us, event | category | flops | bytes accessed | tf_op | source)
XLA Modules:
  0.0 79.5 jit_solution(10262987306328155567)
XLA Ops:
  1.3 75.1 %step.1 = (bf16[448,1008]{1,0:T(8,128)(2,1)S(1)}, bf16[224,126]{1,0:T(8,128)(2,1)S(1)}, f32[126,2016]{1,0:T(8,128)S(1)}, f32[1000,126]{1,0:T(8,128)S(1)}) custom-call(s32[1]{0:T(128)S(6)} %copy.12.label, s32[16]{0:T(128)} %partner_h.1, bf16[224,126]{1,0:T(8,128)(2,1)} %bitcast.32, bf16[9,1008,126]{2,1,0:T(8,128)(2,1)} %bitcast.26, ...), custom_call_target="tpu_custom_call" | custom-call | tf_op jit(solution)/shard_map/step/pallas_call | solution.py:590
  76.4 3.1 %grads.1 = (f32[126,9,1,1008]{3,2,1,0:T(1,128)}, f32[126,1,2016]{2,1,0:T(1,128)}, f32[1000,126]{1,0:T(8,128)}) custom-call(bf16[448,1008]{1,0:T(8,128)(2,1)S(1)} %get-tuple-element.10.xeo, bf16[224,126]{1,0:T(8,128)(2,1)S(1)} %get-tuple-element.11.dpre, f32[126,2016]{1,0:T(8,128)S(1)} %get-tuple-element.12.r1, f32[1000,126]{1,0:T(8,128)S(1)} %get-tuple-element.13.r0), custom_call_target="tpu_custom_call" | custom-call | tf_op jit(solution)/shard_map/grads/pallas_call | solution.py:651

commit v4 on v3

--- a/solution.py
+++ b/solution.py
@@ -48,9 +48,10 @@
 
 
 class Gather:
-    def __init__(self, panel, send, recv, here, parts=1):
+    def __init__(self, panel, send, recv, here, parts=1, ring=False):
         self.panel, self.send, self.recv, self.here = panel, send, recv, here
         self.parts = parts
+        self.ring = ring
         self.started = []
 
     def copy(self, kind, slot, target, part=None):
@@ -85,7 +86,6 @@
         h = self.here
         self.go(1, h.me, h.right)
         self.go(2, h.me, h.left)
-        self.go(5, h.me, h.far)
         self.go(7, h.me, h.sib)
 
     def across(self):
@@ -98,20 +98,36 @@
         h = self.here
         self.go(3, h.opp, h.right, part)
         self.go(4, h.opp, h.left, part)
-        self.go(6, h.opp, h.far, part)
+        if not self.ring:
+            self.go(6, h.opp, h.far, part)
 
     def near(self):
         h = self.here
-        for kind, slot, onward in ((1, h.left, 9), (2, h.right, 10), (5, h.far, 13)):
-            self.got(kind, slot)
-            self.go(onward, slot, h.sib)
+        self.got(2, h.right)
+        self.go(5, h.right, h.left)
+        self.go(10, h.right, h.sib)
+        self.got(1, h.left)
+        self.go(9, h.left, h.sib)
+
+    def far(self):
+        self.got(5, self.here.far)
+        self.go(13, self.here.far, self.here.sib)
 
     def near_opp(self):
         h = self.here
-        for kind, slot, onward in ((3, h.left_opp, 11), (4, h.right_opp, 12), (6, h.far_opp, 14)):
-            for part in range(self.parts):
-                self.got(kind, slot, part)
-            self.go(onward, slot, h.sib)
+        for part in range(self.parts):
+            self.got(3, h.left_opp, part)
+        if self.ring:
+            self.go(6, h.left_opp, h.right)
+        self.go(11, h.left_opp, h.sib)
+        for part in range(self.parts):
+            self.got(4, h.right_opp, part)
+        self.go(12, h.right_opp, h.sib)
+
+    def far_opp(self):
+        for part in range(self.parts):
+            self.got(6, self.here.far_opp, part)
+        self.go(14, self.here.far_opp, self.here.sib)
 
     def plane(self):
         h = self.here
@@ -203,9 +219,9 @@
     perm = perm.astype(BF16)
     pl.semaphore_wait(barrier, N_REP - 1 + N_FILT - 1)
 
-    gx = Gather(xg, gsend.at[0], grecv.at[0], h)
+    gx = Gather(xg, gsend.at[0], grecv.at[0], h, ring=True)
     gxt = Gather(xgt, gsend.at[1], grecv.at[1], h)
-    gh = Gather(hg, gsend.at[2], grecv.at[2], h)
+    gh = Gather(hg, gsend.at[2], grecv.at[2], h, ring=True)
     ght = Gather(hgt, gsend.at[3], grecv.at[3], h, 2)
 
     for i in range(1, N_REP):
@@ -274,6 +290,7 @@
     ordered(w3s, wxs, 4, 8)
     gx.across()
     ordered(w3s, wxs, 8, 9)
+    gx.far()
     loads[3].wait()
     ordered(w3t, wxt, 0, 2)
 
@@ -300,10 +317,17 @@
     def conv_half(panel, wx, acc, z, first):
         rows = pl.ds(pl.multiple_of(z * (8 * LANES), 8 * LANES), 8 * LANES)
         left = jnp.concatenate([panel[z * 8 + i] for i in range(8)], axis=1)
-        for i in range(3):
-            where = slice(i * 3 * LANES, (i + 1) * 3 * LANES)
+
+        def body(where):
             part = mm(left, wx[rows, where])
             acc[:, where] = part if first else acc[:, where] + part
+
+        def step(i, carry):
+            body(pl.ds(pl.multiple_of(i * 4 * LANES, 4 * LANES), 4 * LANES))
+            return carry
+
+        lax.fori_loop(0, 2, step, 0)
+        body(slice(8 * LANES, 9 * LANES))
 
     lanes = lax.broadcasted_iota(jnp.int32, (POS, LANES), 1)
     column = lax.broadcasted_iota(jnp.int32, (POS, LANES), 0) % MAP_W
@@ -334,9 +358,12 @@
     gxt.near()
     gx.near_opp()
     ordered(w3t, wxt, 5, 9)
+    gxt.far()
+    gx.far_opp()
     gx.plane_opp()
     conv_half(xg, wxs, accs, 1 - h.z, False)
     gxt.near_opp()
+    gxt.far_opp()
     pre = conv_end(accs)
     hg[me] = hidden_of(pre)
     gh.own()
@@ -347,7 +374,6 @@
     hgt[me] = hidden_of(conv_end(acct))
     ght.own()
     gh.near()
-    gh.across()
 
     for which in range(2):
         loads[4 + which].wait()
@@ -355,12 +381,17 @@
             w1p[which, f * LANES : f * LANES + LOC, :] = w1raw[which, f * LOC : (f + 1) * LOC, :]
             w1p[which, f * LANES + LOC : (f + 1) * LANES, :] = jnp.zeros((LANES - LOC, LOC), BF16)
 
+    gh.across()
+    ght.near()
+    gh.far()
+    ght.far()
+    ght.across()
     gh.near_opp()
-    ght.near()
-    ght.across()
+    gh.far_opp()
+    ght.near_opp()
+    ght.far_opp()
     gh.plane()
     gh.plane_opp()
-    ght.near_opp()
 
     def whole(panel):
         return jnp.concatenate([panel[i] for i in range(N_FILT)], axis=1)

time: 79.6 us -> 84.2 us (1.058)
  Pallas kernels: 78.2 us -> 82.8 us
    pallas_call x1, Pallas kernels: 75.1 us -> 79.7 us  [per_device(): pl.pallas_call(main_kernel, out_shape=(pltpu.VMEM((2 * POS, GW), BF16), p...]
where the time goes in v4:
time: 84.2 us; the launch traced here: 84.1 us
  Pallas kernels  82.8 us (98%)
  between operations  1.29 us (2%)
    pallas_call x1, Pallas kernels, per_device(): pl.pallas_call(main_kernel, out_shape=(pltpu.VMEM((2 * POS, GW), BF16), p...  79.7 us
    pallas_call x1, Pallas kernels, per_device(): pl.pallas_call(grads_kernel, out_shape=(sds((LOC, 9, 1, GW), F32), sds((L...  3.11 us

profile of v4, /device:TPU:1, one launch (start us, length us, event | category | flops | bytes accessed | tf_op | source)
XLA Modules:
  0.0 84.1 jit_solution(9507969833742989005)
XLA Ops:
  1.3 79.7 %step.1 = (bf16[448,1008]{1,0:T(8,128)(2,1)S(1)}, bf16[224,126]{1,0:T(8,128)(2,1)S(1)}, f32[126,2016]{1,0:T(8,128)S(1)}, f32[1000,126]{1,0:T(8,128)S(1)}) custom-call(s32[1]{0:T(128)S(6)} %copy.12.label, s32[16]{0:T(128)} %partner_h.1, bf16[224,126]{1,0:T(8,128)(2,1)} %bitcast.32, bf16[9,1008,126]{2,1,0:T(8,128)(2,1)} %bitcast.26, ...), custom_call_target="tpu_custom_call" | custom-call | tf_op jit(solution)/shard_map/step/pallas_call | solution.py:621
  81.0 3.1 %grads.1 = (f32[126,9,1,1008]{3,2,1,0:T(1,128)}, f32[126,1,2016]{2,1,0:T(1,128)}, f32[1000,126]{1,0:T(8,128)}) custom-call(bf16[448,1008]{1,0:T(8,128)(2,1)S(1)} %get-tuple-element.10.xeo, bf16[224,126]{1,0:T(8,128)(2,1)S(1)} %get-tuple-element.11.dpre, f32[126,2016]{1,0:T(8,128)S(1)} %get-tuple-element.12.r1, f32[1000,126]{1,0:T(8,128)S(1)} %get-tuple-element.13.r0), custom_call_target="tpu_custom_call" | custom-call | tf_op jit(solution)/shard_map/grads/pallas_call | solution.py:682

commit v5 on v3

--- a/solution.py
+++ b/solution.py
@@ -168,16 +168,6 @@
     h = Here()
     rep, me = h.rep, h.me
 
-    barrier = pltpu.get_barrier_semaphore()
-    for i in range(1, N_REP):
-        pl.semaphore_signal(
-            barrier, inc=1, device_id={"rep": (rep + i) % N_REP, "filt": me}, device_id_type=MESH
-        )
-    for i in range(1, N_FILT):
-        pl.semaphore_signal(
-            barrier, inc=1, device_id={"rep": rep, "filt": (me + i) % N_FILT}, device_id_type=MESH
-        )
-
     loads = [
         pltpu.make_async_copy(src, dst, wsem.at[i])
         for i, (src, dst) in enumerate(
@@ -193,7 +183,19 @@
             )
         )
     ]
-    for load in loads:
+    for load in loads[:2]:
+        load.start()
+    barrier = pltpu.get_barrier_semaphore()
+    for i in range(1, N_REP):
+        pl.semaphore_signal(
+            barrier, inc=1, device_id={"rep": (rep + i) % N_REP, "filt": me}, device_id_type=MESH
+        )
+    for i in range(1, N_FILT):
+        pl.semaphore_signal(
+            barrier, inc=1, device_id={"rep": rep, "filt": (me + i) % N_FILT}, device_id_type=MESH
+        )
+
+    for load in loads[2:]:
         load.start()
 
     lane_from = lax.broadcasted_iota(jnp.int32, (LOC, LANES), 0)
@@ -203,15 +205,15 @@
     perm = perm.astype(BF16)
     pl.semaphore_wait(barrier, N_REP - 1 + N_FILT - 1)
 
-    gx = Gather(xg, gsend.at[0], grecv.at[0], h)
+    gx = Gather(xg, gsend.at[0], grecv.at[0], h, 2)
     gxt = Gather(xgt, gsend.at[1], grecv.at[1], h)
-    gh = Gather(hg, gsend.at[2], grecv.at[2], h)
+    gh = Gather(hg, gsend.at[2], grecv.at[2], h, 2)
     ght = Gather(hgt, gsend.at[3], grecv.at[3], h, 2)
 
     for i in range(1, N_REP):
         q = (rep + i) % N_REP
 
-        @pl.when((q % 2 == 0) & (q < 2 * CHUNKS))
+        @pl.when(q < 2 * CHUNKS)
         def _():
             pltpu.make_async_remote_copy(
                 src_ref=x_h.at[pl.ds(pl.multiple_of(q // 2 * RELAY, RELAY), RELAY)],
@@ -246,7 +248,7 @@
 
         lax.fori_loop(first, last, body, 0)
 
-    relay = (rep % 2 == 0) & (rep < 2 * CHUNKS)
+    relay = rep < 2 * CHUNKS
     chunk = pl.ds(pl.multiple_of(rep % (2 * CHUNKS) // 2 * RELAY, RELAY), RELAY)
     loads[2].wait()
     ordered(w3s, wxs, 0, 4)
@@ -256,8 +258,8 @@
         pltpu.make_async_copy(a1.at[pl.ds(0, 15)], a1.at[pl.ds(0, 15)], arecv.at[0]).wait()
         a1[rep] = x[chunk]
         xraw[0, chunk] = a1[partner[rep]]
-        for i in range(N_REP):
-            p = (rep + i) % N_REP
+        for i in (4, 3, 5, 2, 6, 1, 7, 0):
+            p = (rep + 2 * i) % N_REP
             sb[i] = a1[partner[p]]
             for plane, target in enumerate((h.opp, me)):
                 if i > 0 or plane == 0:
@@ -300,8 +302,8 @@
     def conv_half(panel, wx, acc, z, first):
         rows = pl.ds(pl.multiple_of(z * (8 * LANES), 8 * LANES), 8 * LANES)
         left = jnp.concatenate([panel[z * 8 + i] for i in range(8)], axis=1)
-        for i in range(3):
-            where = slice(i * 3 * LANES, (i + 1) * 3 * LANES)
+        for low in (0, 4, 8):
+            where = slice(low * LANES, min(low + 4, 9) * LANES)
             part = mm(left, wx[rows, where])
             acc[:, where] = part if first else acc[:, where] + part
 
@@ -526,13 +528,13 @@
 
     @pl.when(relay)
     def _():
-        wait_bytes(sb, CHUNKS - 1, asend.at[0])
-        wait_bytes(sb, N_REP, asend.at[1])
-        wait_bytes(sb, N_REP - 1, asend.at[3])
+        wait_bytes(sb, 2 * CHUNKS - 1, asend.at[0])
+        wait_bytes(sb, 8, asend.at[1])
+        wait_bytes(sb, 7, asend.at[3])
 
     @pl.when(jnp.logical_not(relay))
     def _():
-        wait_bytes(sb, CHUNKS, asend.at[0])
+        wait_bytes(sb, 2 * CHUNKS, asend.at[0])
 
 
 def grads_kernel(xeo, dpre, r1, r0, gw3, gw1, gh, turned, r3, sem):
@@ -549,7 +551,7 @@
     even = lax.broadcasted_iota(jnp.int32, (POS, LOC), 1) % 2 == 0
     column = lax.broadcasted_iota(jnp.int32, (POS, LOC), 0) % MAP_W
     zero = jnp.zeros((MAP_W, LOC), F32)
-    for b in range(3):
+    for b in (1, 0, 2):
         moved = dp
         if b == 0:
             moved = pltpu.roll(jnp.where(column >= 1, dp, 0.0), POS - 1, 0)
@@ -564,7 +566,6 @@
             where = slice(a * LANES, a * LANES + LOC)
             turned[b, :POS, where] = jnp.where(even, d, 0.0).astype(BF16)
             turned[b, POS:, where] = jnp.where(even, 0.0, d).astype(BF16)
-    for b in range(3):
         rows = mm(turned[b], xeo[...], ((0,), (0,)))
         for a in range(3):
             t = 3 * a + b

time: 79.6 us -> 79.2 us (level)
  no operation moved by 1% of the time
where the time goes in v5:
time: 79.2 us; the launch traced here: 79.1 us
  Pallas kernels  77.8 us (98%)
  between operations  1.29 us (2%)
    pallas_call x1, Pallas kernels, per_device(): pl.pallas_call(main_kernel, out_shape=(pltpu.VMEM((2 * POS, GW), BF16), p...  74.8 us
    pallas_call x1, Pallas kernels, per_device(): pl.pallas_call(grads_kernel, out_shape=(sds((LOC, 9, 1, GW), F32), sds((L...  3.08 us

profile of v5, /device:TPU:1, one launch (start us, length us, event | category | flops | bytes accessed | tf_op | source)
XLA Modules:
  0.0 79.1 jit_solution(17263491588098157465)
XLA Ops:
  1.3 74.8 %step.1 = (bf16[448,1008]{1,0:T(8,128)(2,1)S(1)}, bf16[224,126]{1,0:T(8,128)(2,1)S(1)}, f32[126,2016]{1,0:T(8,128)S(1)}, f32[1000,126]{1,0:T(8,128)S(1)}) custom-call(s32[1]{0:T(128)S(6)} %copy.12.label, s32[16]{0:T(128)} %partner_h.1, bf16[224,126]{1,0:T(8,128)(2,1)} %bitcast.32, bf16[9,1008,126]{2,1,0:T(8,128)(2,1)} %bitcast.26, ...), custom_call_target="tpu_custom_call" | custom-call | tf_op jit(solution)/shard_map/step/pallas_call | solution.py:591
  76.1 3.1 %grads.1 = (f32[126,9,1,1008]{3,2,1,0:T(1,128)}, f32[126,1,2016]{2,1,0:T(1,128)}, f32[1000,126]{1,0:T(8,128)}) custom-call(bf16[448,1008]{1,0:T(8,128)(2,1)S(1)} %get-tuple-element.10.xeo, bf16[224,126]{1,0:T(8,128)(2,1)S(1)} %get-tuple-element.11.dpre, f32[126,2016]{1,0:T(8,128)S(1)} %get-tuple-element.12.r1, f32[1000,126]{1,0:T(8,128)S(1)} %get-tuple-element.13.r0), custom_call_target="tpu_custom_call" | custom-call | tf_op jit(solution)/shard_map/grads/pallas_call | solution.py:652

commit v6 on v5

--- a/solution.py
+++ b/solution.py
@@ -161,7 +161,7 @@
 def main_kernel(
     label, partner_h, x_h, w3s_h, w1s_h, hds_h, w3t_h, w1t_h, hdt_h,
     xeo, dpre_out, gw1_out, gh_out,
-    partner, x, xraw, hc, w3s, w3t, wxs, wxt, w1raw, w1p, hds, hdt, xg, xgt, hg, hgt, accs, acct,
+    partner, x, xraw, xeot, hc, w3s, w3t, wxs, wxt, w1raw, w1p, hds, hdt, xg, xgt, hg, hgt, accs, acct,
     a1, sb, ls, lt, ua, row, sendb, block, ra, rb, rc,
     wsem, gsend, grecv, asend, arecv, lsend, lrecv, rsend, rrecv,
 ):
@@ -229,29 +229,14 @@
     gx.own()
     loads[1].wait()
 
-    def ordered(w3, wx, first, last):
-        keep = lax.broadcasted_iota(jnp.int32, (64, LOC), 0) < HALF
-        even = lax.broadcasted_iota(jnp.int32, (64, LOC), 1) % 2 == 0
-
-        def body(t, carry):
-            where = pl.ds(pl.multiple_of(t * LANES, LANES), LOC)
-            w = jnp.concatenate([w3[t].astype(F32), jnp.zeros((8, LOC), F32)], axis=0)
-            for f in range(N_FILT):
-                piece = w[f * HALF : f * HALF + 64]
-                wx[f * LANES : f * LANES + 64, where] = jnp.where(
-                    keep & even, piece, 0.0
-                ).astype(BF16)
-                wx[f * LANES + 64 : (f + 1) * LANES, where] = jnp.where(
-                    keep & ~even, piece, 0.0
-                ).astype(BF16)
-            return carry
-
-        lax.fori_loop(first, last, body, 0)
+    def pack(w3, wx):
+        for t in range(9):
+            wx[:, t * LANES : t * LANES + LOC] = w3[t]
 
     relay = rep < 2 * CHUNKS
     chunk = pl.ds(pl.multiple_of(rep % (2 * CHUNKS) // 2 * RELAY, RELAY), RELAY)
     loads[2].wait()
-    ordered(w3s, wxs, 0, 4)
+    pack(w3s, wxs)
 
     @pl.when(relay)
     def _():
@@ -273,11 +258,9 @@
                     ).start()
 
     gx.near()
-    ordered(w3s, wxs, 4, 8)
     gx.across()
-    ordered(w3s, wxs, 8, 9)
     loads[3].wait()
-    ordered(w3t, wxt, 0, 2)
+    pack(w3t, wxt)
 
     @pl.when(relay)
     def _():
@@ -297,15 +280,24 @@
     xgt[h.opp] = mm(xraw[1], perm).astype(BF16)
     gxt.spread_opp(0)
     gxt.go(8, h.opp, h.sib)
-    ordered(w3t, wxt, 2, 5)
-
-    def conv_half(panel, wx, acc, z, first):
-        rows = pl.ds(pl.multiple_of(z * (8 * LANES), 8 * LANES), 8 * LANES)
-        left = jnp.concatenate([panel[z * 8 + i] for i in range(8)], axis=1)
+
+    def assemble(panel, out, z):
+        for plane in range(2):
+
+            @pl.when(z == plane)
+            def _():
+                for f in range(plane * 8, plane * 8 + 8):
+                    for g in range(2):
+                        out[g * POS : (g + 1) * POS, f * HALF : (f + 1) * HALF] = panel[
+                            f, :, 64 * g : 64 * g + HALF
+                        ]
+
+    def conv(panel, wx, acc):
         for low in (0, 4, 8):
             where = slice(low * LANES, min(low + 4, 9) * LANES)
-            part = mm(left, wx[rows, where])
-            acc[:, where] = part if first else acc[:, where] + part
+            both = mm(panel[...], wx[:, where])
+            even = lax.broadcasted_iota(jnp.int32, (POS, both.shape[1]), 1) % 2 == 0
+            acc[:, where] = jnp.where(even, both[:POS], both[POS:])
 
     lanes = lax.broadcasted_iota(jnp.int32, (POS, LANES), 1)
     column = lax.broadcasted_iota(jnp.int32, (POS, LANES), 0) % MAP_W
@@ -332,20 +324,21 @@
         return jnp.where(lanes < LOC, silu(pre), 0.0).astype(BF16)
 
     gx.plane()
-    conv_half(xg, wxs, accs, h.z, True)
+    assemble(xg, xeo, h.z)
     gxt.near()
     gx.near_opp()
-    ordered(w3t, wxt, 5, 9)
     gx.plane_opp()
-    conv_half(xg, wxs, accs, 1 - h.z, False)
+    assemble(xg, xeo, 1 - h.z)
+    conv(xeo, wxs, accs)
     gxt.near_opp()
     pre = conv_end(accs)
     hg[me] = hidden_of(pre)
     gh.own()
     gxt.plane()
-    conv_half(xgt, wxt, acct, h.z, True)
+    assemble(xgt, xeot, h.z)
     gxt.plane_opp()
-    conv_half(xgt, wxt, acct, 1 - h.z, False)
+    assemble(xgt, xeot, 1 - h.z)
+    conv(xeot, wxt, acct)
     hgt[me] = hidden_of(conv_end(acct))
     ght.own()
     gh.near()
@@ -432,11 +425,6 @@
             device_id={"rep": (rep + i) % N_REP, "filt": me},
             device_id_type=MESH,
         ).start()
-    for f in range(N_FILT):
-        for g in range(2):
-            xeo[g * POS : (g + 1) * POS, f * HALF : (f + 1) * HALF] = xg[
-                f, :, 64 * g : 64 * g + HALF
-            ]
     wait_bytes(ua, N_REP - 1, arecv.at[2])
     dl = own_part - softmax(ua[partner[rep]])
     dl_row = jnp.concatenate([dl[i : i + 1, :] for i in range(8)], axis=1)[:, :K]
@@ -602,11 +590,12 @@
             pltpu.SMEM((N_REP,), jnp.int32),
             pltpu.VMEM((POS, LOC), BF16),
             pltpu.VMEM((2, POS, LOC), BF16),
+            pltpu.VMEM((2 * POS, GW), BF16),
             pltpu.VMEM((POS, C), BF16),
             pltpu.VMEM((9, GW, LOC), BF16),
             pltpu.VMEM((9, GW, LOC), BF16),
-            pltpu.VMEM((N_FILT * LANES, 9 * LANES), BF16),
-            pltpu.VMEM((N_FILT * LANES, 9 * LANES), BF16),
+            pltpu.VMEM((GW, 9 * LANES), BF16),
+            pltpu.VMEM((GW, 9 * LANES), BF16),
             pltpu.VMEM((2, C, LOC), BF16),
             pltpu.VMEM((2, N_FILT * LANES, LOC), BF16),
             pltpu.VMEM((K, LOC), BF16),

time: 79.2 us -> 80.1 us (1.011)
  no operation moved by 1% of the time
where the time goes in v6:
time: 80.1 us; the launch traced here: 80 us
  Pallas kernels  78.5 us (98%)
  between operations  1.45 us (2%)
    pallas_call x1, Pallas kernels, per_device(): pl.pallas_call(main_kernel, out_shape=(pltpu.VMEM((2 * POS, GW), BF16), p...  75.5 us
    pallas_call x1, Pallas kernels, per_device(): pl.pallas_call(grads_kernel, out_shape=(sds((LOC, 9, 1, GW), F32), sds((L...  3.08 us

profile of v6, /device:TPU:1, one launch (start us, length us, event | category | flops | bytes accessed | tf_op | source)
XLA Modules:
  0.0 80.0 jit_solution(4267758123919889811)
XLA Ops:
  1.3 75.5 %step.1 = (bf16[448,1008]{1,0:T(8,128)(2,1)S(1)}, bf16[224,126]{1,0:T(8,128)(2,1)S(1)}, f32[126,2016]{1,0:T(8,128)S(1)}, f32[1000,126]{1,0:T(8,128)S(1)}) custom-call(s32[1]{0:T(128)S(6)} %copy.12.label, s32[16]{0:T(128)} %partner_h.1, bf16[224,126]{1,0:T(8,128)(2,1)} %bitcast.32, bf16[9,1008,126]{2,1,0:T(8,128)(2,1)} %bitcast.26, ...), custom_call_target="tpu_custom_call" | custom-call | tf_op jit(solution)/shard_map/step/pallas_call | solution.py:579
  76.7 3.1 %grads.1 = (f32[126,9,1,1008]{3,2,1,0:T(1,128)}, f32[126,1,2016]{2,1,0:T(1,128)}, f32[1000,126]{1,0:T(8,128)}) custom-call(bf16[448,1008]{1,0:T(8,128)(2,1)S(1)} %get-tuple-element.10.xeo, bf16[224,126]{1,0:T(8,128)(2,1)S(1)} %get-tuple-element.11.dpre, f32[126,2016]{1,0:T(8,128)S(1)} %get-tuple-element.12.r1, f32[1000,126]{1,0:T(8,128)S(1)} %get-tuple-element.13.r0), custom_call_target="tpu_custom_call" | custom-call | tf_op jit(solution)/shard_map/grads/pallas_call | solution.py:641

commit v7 on v5

--- a/solution.py
+++ b/solution.py
@@ -357,15 +357,20 @@
             w1p[which, f * LANES : f * LANES + LOC, :] = w1raw[which, f * LOC : (f + 1) * LOC, :]
             w1p[which, f * LANES + LOC : (f + 1) * LANES, :] = jnp.zeros((LANES - LOC, LOC), BF16)
 
+    for f in range(N_FILT):
+        for g in range(2):
+            xeo[g * POS : (g + 1) * POS, f * HALF : (f + 1) * HALF] = xg[
+                f, :, 64 * g : 64 * g + HALF
+            ]
     gh.near_opp()
     ght.near()
     ght.across()
-    gh.plane()
-    gh.plane_opp()
     ght.near_opp()
 
-    def whole(panel):
-        return jnp.concatenate([panel[i] for i in range(N_FILT)], axis=1)
+    def mixed(panel, which, z):
+        rows = pl.ds(pl.multiple_of(z * 8 * LANES, 8 * LANES), 8 * LANES)
+        left = jnp.concatenate([panel[z * 8 + i] for i in range(8)], axis=1)
+        return mm(left, w1p[which, rows, :])
 
     def logits_of(z, head):
         pooled = jnp.sum(silu(z), axis=0, keepdims=True) * (1.0 / POS)
@@ -398,30 +403,16 @@
 
     loads[6].wait()
     loads[7].wait()
-    z_mixed = x[...].astype(F32) + mm(whole(hg), w1p[0])
+    ght.plane()
+    zt = xraw[0].astype(F32) + mixed(hgt, 1, h.z)
+    ght.plane_opp()
+    part = logits_of(zt + mixed(hgt, 1, 1 - h.z), hdt)[1]
+    give_logits(lt, part, 1)
+    gh.plane()
+    gh.plane_opp()
+    z_mixed = x[...].astype(F32) + mixed(hg, 0, h.z) + mixed(hg, 0, 1 - h.z)
     pooled, part = logits_of(z_mixed, hds)
     give_logits(ls, part, 0)
-    xt = xraw[0].astype(F32)
-    ght.plane()
-    ght.plane_opp()
-    part = logits_of(xt + mm(whole(hgt), w1p[1]), hdt)[1]
-    give_logits(lt, part, 1)
-    for f in range(N_FILT):
-        hc[:, f * LOC : (f + 1) * LOC] = hg[f, :, :LOC]
-    logits = sum_logits(ls, 0)
-
-    cls = lax.broadcasted_iota(jnp.int32, (8, LANES), 0) * LANES + lax.broadcasted_iota(
-        jnp.int32, (8, LANES), 1
-    )
-    real = cls < K
-
-    def softmax(v):
-        top = jnp.max(jnp.where(real, v, -jnp.inf))
-        e = jnp.where(real, jnp.exp(v - top), 0.0)
-        return e / jnp.sum(e)
-
-    own_part = 2.0 * softmax(logits) - jnp.where(cls == label[0], 1.0, 0.0)
-    slope = dsilu(z_mixed) * (1.0 / POS)
     ua[rep] = sum_logits(lt, 1)
     for i in range(1, N_REP):
         pltpu.make_async_remote_copy(
@@ -432,11 +423,20 @@
             device_id={"rep": (rep + i) % N_REP, "filt": me},
             device_id_type=MESH,
         ).start()
-    for f in range(N_FILT):
-        for g in range(2):
-            xeo[g * POS : (g + 1) * POS, f * HALF : (f + 1) * HALF] = xg[
-                f, :, 64 * g : 64 * g + HALF
-            ]
+    slope = dsilu(z_mixed) * (1.0 / POS)
+    logits = sum_logits(ls, 0)
+
+    cls = lax.broadcasted_iota(jnp.int32, (8, LANES), 0) * LANES + lax.broadcasted_iota(
+        jnp.int32, (8, LANES), 1
+    )
+    real = cls < K
+
+    def softmax(v):
+        top = jnp.max(jnp.where(real, v, -jnp.inf))
+        e = jnp.where(real, jnp.exp(v - top), 0.0)
+        return e / jnp.sum(e)
+
+    own_part = 2.0 * softmax(logits) - jnp.where(cls == label[0], 1.0, 0.0)
     wait_bytes(ua, N_REP - 1, arecv.at[2])
     dl = own_part - softmax(ua[partner[rep]])
     dl_row = jnp.concatenate([dl[i : i + 1, :] for i in range(8)], axis=1)[:, :K]
@@ -507,6 +507,8 @@
     for j in (1, 2, 0):
         across[6 + j].wait_recv()
         mine = mine + rb[3 + j].astype(F32)
+    for f in range(N_FILT):
+        hc[:, f * LOC : (f + 1) * LOC] = hg[f, :, :LOC]
     gw1_out[...] = mm(dz, hc[...], ((0,), (0,)))
     flip = dl.T
     for i in range(8):

time: 79.2 us -> 79.7 us (level)
  no operation moved by 1% of the time
where the time goes in v7:
time: 79.7 us; the launch traced here: 79.6 us
  Pallas kernels  78.3 us (98%)
  between operations  1.29 us (2%)
    pallas_call x1, Pallas kernels, per_device(): pl.pallas_call(main_kernel, out_shape=(pltpu.VMEM((2 * POS, GW), BF16), p...  75.2 us
    pallas_call x1, Pallas kernels, per_device(): pl.pallas_call(grads_kernel, out_shape=(sds((LOC, 9, 1, GW), F32), sds((L...  3.08 us

profile of v7, /device:TPU:1, one launch (start us, length us, event | category | flops | bytes accessed | tf_op | source)
XLA Modules:
  0.0 79.6 jit_solution(4724498031293006366)
XLA Ops:
  1.3 75.2 %step.1 = (bf16[448,1008]{1,0:T(8,128)(2,1)S(1)}, bf16[224,126]{1,0:T(8,128)(2,1)S(1)}, f32[126,2016]{1,0:T(8,128)S(1)}, f32[1000,126]{1,0:T(8,128)S(1)}) custom-call(s32[1]{0:T(128)S(6)} %copy.12.label, s32[16]{0:T(128)} %partner_h.1, bf16[224,126]{1,0:T(8,128)(2,1)} %bitcast.32, bf16[9,1008,126]{2,1,0:T(8,128)(2,1)} %bitcast.26, ...), custom_call_target="tpu_custom_call" | custom-call | tf_op jit(solution)/shard_map/step/pallas_call | solution.py:593
  76.5 3.1 %grads.1 = (f32[126,9,1,1008]{3,2,1,0:T(1,128)}, f32[126,1,2016]{2,1,0:T(1,128)}, f32[1000,126]{1,0:T(8,128)}) custom-call(bf16[448,1008]{1,0:T(8,128)(2,1)S(1)} %get-tuple-element.10.xeo, bf16[224,126]{1,0:T(8,128)(2,1)S(1)} %get-tuple-element.11.dpre, f32[126,2016]{1,0:T(8,128)S(1)} %get-tuple-element.12.r1, f32[1000,126]{1,0:T(8,128)S(1)} %get-tuple-element.13.r0), custom_call_target="tpu_custom_call" | custom-call | tf_op jit(solution)/shard_map/grads/pallas_call | solution.py:654

commit v8 on v5

--- a/solution.py
+++ b/solution.py
@@ -48,9 +48,10 @@
 
 
 class Gather:
-    def __init__(self, panel, send, recv, here, parts=1):
+    def __init__(self, panel, send, recv, here, parts=1, both=False):
         self.panel, self.send, self.recv, self.here = panel, send, recv, here
         self.parts = parts
+        self.both = both
         self.started = []
 
     def copy(self, kind, slot, target, part=None):
@@ -58,7 +59,7 @@
         if part is not None and self.parts > 1:
             size = POS // self.parts
             where = self.panel.at[slot, pl.ds(part * size, size)]
-            kind = kind if part == 0 else 15 + (0, 3, 4, 6).index(kind)
+            kind = kind if part == 0 else 15 + (0, 3, 4, 6, 11, 12, 14).index(kind)
         return pltpu.make_async_remote_copy(
             src_ref=where,
             dst_ref=where,
@@ -99,6 +100,10 @@
         self.go(3, h.opp, h.right, part)
         self.go(4, h.opp, h.left, part)
         self.go(6, h.opp, h.far, part)
+        if self.both:
+            self.go(11, h.opp, h.other(h.right), part)
+            self.go(12, h.opp, h.other(h.left), part)
+            self.go(14, h.opp, h.other(h.far), part)
 
     def near(self):
         h = self.here
@@ -111,7 +116,8 @@
         for kind, slot, onward in ((3, h.left_opp, 11), (4, h.right_opp, 12), (6, h.far_opp, 14)):
             for part in range(self.parts):
                 self.got(kind, slot, part)
-            self.go(onward, slot, h.sib)
+            if not self.both:
+                self.go(onward, slot, h.sib)
 
     def plane(self):
         h = self.here
@@ -123,9 +129,9 @@
     def plane_opp(self):
         h = self.here
         self.got(8, h.other(h.opp))
-        self.got(11, h.other(h.left_opp))
-        self.got(12, h.other(h.right_opp))
-        self.got(14, h.other(h.far_opp))
+        for kind, slot in ((11, h.left_opp), (12, h.right_opp), (14, h.far_opp)):
+            for part in range(self.parts) if self.both else (None,):
+                self.got(kind, h.other(slot), part)
 
     def drain(self):
         for made in self.started:
@@ -206,9 +212,9 @@
     pl.semaphore_wait(barrier, N_REP - 1 + N_FILT - 1)
 
     gx = Gather(xg, gsend.at[0], grecv.at[0], h, 2)
-    gxt = Gather(xgt, gsend.at[1], grecv.at[1], h)
+    gxt = Gather(xgt, gsend.at[1], grecv.at[1], h, 1, True)
     gh = Gather(hg, gsend.at[2], grecv.at[2], h, 2)
-    ght = Gather(hgt, gsend.at[3], grecv.at[3], h, 2)
+    ght = Gather(hgt, gsend.at[3], grecv.at[3], h, 2, True)
 
     for i in range(1, N_REP):
         q = (rep + i) % N_REP
@@ -629,8 +635,8 @@
             pltpu.VMEM((6, POS, LANES), BF16),
             pltpu.VMEM((POS, LANES), BF16),
             dma((8,)),
-            dma((4, 19)),
-            dma((4, 19)),
+            dma((4, 22)),
+            dma((4, 22)),
             dma((4,)),
             dma((4,)),
             dma((2,)),

time: 79.2 us -> 81.2 us (1.025)
  Pallas kernels: 77.8 us -> 79.8 us
    pallas_call x1, Pallas kernels: 74.8 us -> 76.8 us  [per_device(): pl.pallas_call(main_kernel, out_shape=(pltpu.VMEM((2 * POS, GW), BF16), p...]
where the time goes in v8:
time: 81.2 us; the launch traced here: 81.1 us
  Pallas kernels  79.8 us (98%)
  between operations  1.29 us (2%)
    pallas_call x1, Pallas kernels, per_device(): pl.pallas_call(main_kernel, out_shape=(pltpu.VMEM((2 * POS, GW), BF16), p...  76.8 us
    pallas_call x1, Pallas kernels, per_device(): pl.pallas_call(grads_kernel, out_shape=(sds((LOC, 9, 1, GW), F32), sds((L...  3.08 us

profile of v8, /device:TPU:1, one launch (start us, length us, event | category | flops | bytes accessed | tf_op | source)
XLA Modules:
  0.0 81.1 jit_solution(9766086777363257262)
XLA Ops:
  1.3 76.8 %step.1 = (bf16[448,1008]{1,0:T(8,128)(2,1)S(1)}, bf16[224,126]{1,0:T(8,128)(2,1)S(1)}, f32[126,2016]{1,0:T(8,128)S(1)}, f32[1000,126]{1,0:T(8,128)S(1)}) custom-call(s32[1]{0:T(128)S(6)} %copy.12.label, s32[16]{0:T(128)} %partner_h.1, bf16[224,126]{1,0:T(8,128)(2,1)} %bitcast.32, bf16[9,1008,126]{2,1,0:T(8,128)(2,1)} %bitcast.26, ...), custom_call_target="tpu_custom_call" | custom-call | tf_op jit(solution)/shard_map/step/pallas_call | solution.py:597
  78.0 3.1 %grads.1 = (f32[126,9,1,1008]{3,2,1,0:T(1,128)}, f32[126,1,2016]{2,1,0:T(1,128)}, f32[1000,126]{1,0:T(8,128)}) custom-call(bf16[448,1008]{1,0:T(8,128)(2,1)S(1)} %get-tuple-element.10.xeo, bf16[224,126]{1,0:T(8,128)(2,1)S(1)} %get-tuple-element.11.dpre, f32[126,2016]{1,0:T(8,128)S(1)} %get-tuple-element.12.r1, f32[1000,126]{1,0:T(8,128)S(1)} %get-tuple-element.13.r0), custom_call_target="tpu_custom_call" | custom-call | tf_op jit(solution)/shard_map/grads/pallas_call | solution.py:658
